TPU v7x, 256 devices: a whole 4x4x8 slice. The times are simulated.
256 devices in a mesh: head: 8 (over y_lo, x), ctx: 32 (over z, y_hi, core).
Axes of the slice: x: 4, y: 4 (y_hi: 2, y_lo: 2; y = y_hi * 2 + y_lo), z: 8, core: 2. Of those that a mesh axis runs over, the one named last changes fastest.
Arguments:
- queries: bfloat16 [2048, 8192], P('ctx', 'head'), may hold values from -102 to 102
- latent_keys: bfloat16 [32768, 1024], P('ctx', 'head'), may hold values from -6 to 6
- latent_values: bfloat16 [32768, 1024], P('ctx', 'head'), may hold values from -6 to 6
- key_basis: bfloat16 [8, 128, 128], P('head'), may hold values from -0.5 to 0.5
- value_basis: bfloat16 [8, 128, 128], P('head'), may hold values from -0.5 to 0.5
- out_weight: bfloat16 [8192, 8192], P('head', 'ctx'), may hold values from -0.0625 to 0.0625
- positions: int32 [2048], replicated, may hold values from 0 to 32767, as said below
- key_segments: int32 [32768], replicated, may hold values from 0 to 1, as said below
Outputs:
- scored: bfloat16 [2048, 8192], P('head', 'ctx')
Inputs may be any that keep to these rules, and one draw needn't show every extreme that they name: `positions`: strictly rising; rows c*64 to (c+1)*64 - 1 hold positions in c*1024 to (c+1)*1024 - 1. `key_segments`: never falling; each of the 2 values names one nonempty run of tokens.
All inputs are finite; a program needn't handle non-finite values.
Results may differ from a plain program's by a relative error of at most 0.012.
The roundings to bfloat16 on the way count: a program that leaves them out, or rounds other values in their place, can miss the bound.
Values may be sent and summed in bfloat16 or wider, within the bound.
No kernel may reach another device: no remote copies, remote signals or barrier semaphores. Data moves between devices by JAX's collectives and lax.ppermute only.
A program may use at most 128 MiB of HBM per device.

v0:
```python
import functools
import math

import jax
import jax.numpy as jnp
import numpy as np
from jax import lax
from jax.experimental import pallas as pl
from jax.experimental.pallas import tpu as pltpu
from jax.sharding import Mesh, PartitionSpec as P

NZ = 8
LAST = NZ - 1
NOWHERE = 1 << 16
FLOOR = -1e30
MASKED = -2e38
CLIMB = 40.0
F32 = jnp.float32
BF16 = jnp.bfloat16
VMEM = pl.BlockSpec(memory_space=pltpu.VMEM)
SMEM = pl.BlockSpec(memory_space=pltpu.SMEM)
ANY = pl.BlockSpec(memory_space=pl.ANY)
LIMIT = 24 * 1024 * 1024
FLASH_LIMIT = 40 * 1024 * 1024
REBUILD_LIMIT = 60 * 1024 * 1024
SHIFTS = (0, 2, 6, 4)


def cost(flops, moved):
    return pl.CostEstimate(flops=int(flops), bytes_accessed=int(moved), transcendentals=0)


def rebuild_kernel(lk_in, lv_in, bk_in, bv_in, kv_ref, lk_ref, lv_ref, bk_ref, bv_ref, sems):
    pairs = [(lk_in, lk_ref), (bk_in, bk_ref), (lv_in, lv_ref), (bv_in, bv_ref)]
    copies = [pltpu.make_async_copy(a, b, sems.at[n]) for n, (a, b) in enumerate(pairs)]
    for c in copies:
        c.start()
    for c in copies:
        c.wait()
    hd = bk_ref.shape[2]
    values = lax.dot_general(
        bv_ref[0], lv_ref[...], (((0,), (1,)), ((), ())), preferred_element_type=F32
    )
    kv_ref[:hd, :] = values.astype(BF16)
    for t in range(lk_ref.shape[0] // hd):
        part = slice(t * hd, (t + 1) * hd)
        keys = jnp.dot(lk_ref[part, :], bk_ref[0], preferred_element_type=F32)
        kv_ref[hd:, part] = keys.astype(BF16)


def rebuild(lk, lv, bk, bv):
    rows, hd = lk.shape[0], bk.shape[2]
    arrays = (lk, lv, bk, bv)
    return pl.pallas_call(
        rebuild_kernel,
        out_shape=jax.ShapeDtypeStruct((2 * hd, rows), BF16),
        in_specs=[ANY] * 4,
        out_specs=VMEM,
        scratch_shapes=[pltpu.VMEM(t.shape, t.dtype) for t in arrays]
        + [pltpu.SemaphoreType.DMA((4,))],
        compiler_params=pltpu.CompilerParams(vmem_limit_bytes=REBUILD_LIMIT),
        cost_estimate=cost(4 * rows * hd * hd, 8 * rows * hd),
    )(*arrays)


def flash_kernel(nq, nk, first, last, groups, rows, scale2, *refs):
    seg_in, pos_in = refs[0], refs[1]
    qs = refs[2 : 2 + nq]
    spare = refs[2 + nq]
    kvs = refs[3 + nq : 3 + nq + nk]
    at = 3 + nq + nk
    z, yh, core = lax.axis_index("z"), lax.axis_index("yh"), lax.axis_index("core")
    if not first:
        held = refs[at : at + 3 * nq]
        at += 3 * nq
    if last:
        outs = refs[at : at + nq]
        at += nq
    else:
        outs = refs[at : at + 3 * nq]
        at += 3 * nq
    flat_s, q_s, kv_s, pos_s, acc_t, begun, todo, m_s, l_s, acc_s, *rest = refs[at:]
    q_sem, kv_sem, st_sem, seg_ref, pos_ref, small_sem = rest
    hd = kvs[0].shape[0] // 2
    span = kvs[0].shape[1]
    tokens = qs[0].shape[0]
    kv_copies = [pltpu.make_async_copy(kvs[j], kv_s.at[j], kv_sem.at[j]) for j in range(nk)]
    q_copies = [pltpu.make_async_copy(qs[i], flat_s.at[i], q_sem.at[i]) for i in range(nq)]
    small = [
        pltpu.make_async_copy(seg_in, seg_ref, small_sem.at[0]),
        pltpu.make_async_copy(pos_in, pos_ref, small_sem.at[1]),
    ]
    for c in small + q_copies[:1] + q_copies[2:] + kv_copies:
        c.start()

    @pl.when(z == LAST - 1)
    def _():
        pltpu.make_async_copy(spare, flat_s.at[1], q_sem.at[1]).start()

    @pl.when(z != LAST - 1)
    def _():
        q_copies[1].start()

    if first:
        m_s[...] = jnp.full_like(m_s, FLOOR)
        l_s[...] = jnp.zeros_like(l_s)
        acc_s[...] = jnp.zeros_like(acc_s)
    else:
        held_copies = [
            pltpu.make_async_copy(r, (m_s, l_s, acc_s)[n % 3].at[n // 3], st_sem.at[n])
            for n, r in enumerate(held)
        ]
        for c in held_copies:
            c.start()
    for c in small:
        c.wait()
    cut = jnp.sum(jnp.where(seg_ref[...] == 0, 1.0, 0.0)).astype(jnp.int32)

    def query_block(i):
        plane = (z + SHIFTS[i]) & (NZ - 1)
        if i == 1:
            plane = jnp.where(z == LAST - 1, LAST, plane)
        return 4 * plane + 2 * yh + core

    def key_block(j):
        c = core ^ (j & 1)
        above = jnp.where(z == LAST - 2, NOWHERE, (z + 1) & (NZ - 1))
        below = jnp.where(z == LAST, 0, jnp.where(z < 2, NOWHERE, z - 1))
        beside = jnp.where(c == 0, above, below)
        if not first:
            return 4 * beside + 2 * (yh ^ 1) + c
        return 4 * jnp.where(j < 4, z, beside) + 2 * (yh ^ ((j >> 1) & 1)) + c

    for i in range(nq):
        block = query_block(i)
        per = pos_ref.shape[1] // tokens
        line = pos_ref[pl.ds(block // per, 1), :]
        row = line[:, :tokens]
        for n in range(1, per):
            row = jnp.where(block % per == n, line[:, n * tokens : (n + 1) * tokens], row)
        pos_s[i] = jnp.broadcast_to(jnp.concatenate([row] * groups, axis=1), (8, rows))
    for i in range(nq):
        q_copies[i].wait()
        for g in range(groups):
            q_s[i, g * tokens : (g + 1) * tokens, :] = flat_s[i, :, g * hd : (g + 1) * hd]
    if not first:
        for c in held_copies:
            c.wait()

    def scores_of(i, j, step):
        out = []
        for t in range(0, span, step):
            k = jnp.concatenate(
                [kv_s[j, hd:, u : u + hd] for u in range(t, t + step, hd)], axis=0
            )
            out.append(
                lax.dot_general(k, q_s[i], (((1,), (1,)), ((), ())), preferred_element_type=F32)
            )
        return out

    def safe_unit(i, j, ck):
        (s,) = scores_of(i, j, span)
        kpos = lax.broadcasted_iota(jnp.int32, (span, rows), 0) + ck * span
        pos = pos_s[i, :1, :]
        low = jnp.where(pos >= cut, cut, 0)
        s = jnp.where((kpos <= pos) & (kpos >= low), s, MASKED)
        s = s.reshape(span // 8, 8, rows)
        m_old = m_s[i]
        m_new = jnp.maximum(m_old, jnp.max(jnp.max(s, axis=0), axis=0, keepdims=True))
        fade = jnp.exp2((m_old - m_new) * scale2)
        p = jnp.exp2(s * scale2 - (m_new * scale2)[None])
        l_s[i] = l_s[i] * fade + jnp.sum(p, axis=0)
        acc_s[i] = acc_s[i] * fade[:1] + jnp.dot(
            kv_s[j, :hd, :], p.reshape(span, rows).astype(BF16), preferred_element_type=F32
        )
        m_s[i] = m_new

    def fast_unit(i, j):
        step = 2 * hd
        m_old = m_s[i]
        base = m_old * scale2
        top = m_old
        total = l_s[i]
        parts = []
        for s in scores_of(i, j, step):
            s = s.reshape(step // 8, 8, rows)
            top = jnp.maximum(top, jnp.max(s, axis=0))
            p = jnp.exp2(s * scale2 - base[None])
            total = total + jnp.sum(p, axis=0)
            parts.append(p.reshape(step, rows).astype(BF16))
        acc_t[...] = acc_s[i] + jnp.dot(
            kv_s[j, :hd, :], jnp.concatenate(parts, axis=0), preferred_element_type=F32
        )
        m_new = jnp.broadcast_to(jnp.max(top, axis=0, keepdims=True), (8, rows))
        climb = (m_new - m_old) * scale2
        fine = jnp.max(climb) < CLIMB

        @pl.when(fine)
        def _():
            fade = jnp.exp2(-climb)
            l_s[i] = total * fade
            acc_s[i] = acc_t[...] * fade[:1]
            m_s[i] = m_new

        return fine

    for i in range(nq):
        begun[i] = (jnp.max(m_s[i]) > 0.5 * FLOOR).astype(jnp.int32) if not first else jnp.int32(0)

    def one(n, carry):
        j = n // nq
        i = n % nq
        ck = key_block(j)
        cq = query_block(0)
        for n in range(1, nq):
            cq = jnp.where(i == n, query_block(n), cq)
        lent = (i == 1) & (z == LAST - 1)
        cq = jnp.where(lent & (j >= 4 if first else True), -1, cq)
        begin_k, end_k = ck * span, (ck + 1) * span
        begin_q, end_q = cq * span, (cq + 1) * span
        apart = (cut >= end_k) & (cut <= begin_q)
        whole = (ck < cq) & ((cut <= begin_k) | (cut >= end_q))
        some = (ck <= cq) & jnp.logical_not(apart)
        todo[0] = some.astype(jnp.int32)

        @pl.when(i == 0)
        def _():
            pltpu.make_async_copy(kv_s.at[j], kv_s.at[j], kv_sem.at[j]).wait()

        @pl.when(whole & (begun[i] == 0))
        def _():
            s = lax.dot_general(
                kv_s[j, hd:, :hd], q_s[i], (((1,), (1,)), ((), ())), preferred_element_type=F32
            )
            m_s[i] = jnp.broadcast_to(jnp.max(s, axis=0, keepdims=True), (8, rows))
            begun[i] = 1

        @pl.when(whole)
        def _():
            todo[0] = 1 - fast_unit(i, j).astype(jnp.int32)

        @pl.when(todo[0] > 0)
        def _():
            safe_unit(i, j, ck)
            begun[i] = 1

        return carry

    lax.fori_loop(0, nq * nk, one, 0)
    if not last:
        out_copies = [
            pltpu.make_async_copy((m_s, l_s, acc_s)[n % 3].at[n // 3], r, st_sem.at[n])
            for n, r in enumerate(outs)
        ]
        for c in out_copies:
            c.start()
        for c in out_copies:
            c.wait()
        return
    lane = lax.broadcasted_iota(jnp.int32, (tokens, hd), 1)
    for i in range(nq):
        total = jnp.sum(l_s[i], axis=0, keepdims=True)
        used = total > 0.0
        safe = jnp.where(used, total, 1.0)
        done = acc_s[i] * (1.0 / safe)
        level = jnp.where(used, m_s[i, :1, :] * scale2 + jnp.log2(safe), FLOOR)
        high = level.astype(BF16).astype(F32)
        mid = (level - high).astype(BF16).astype(F32)
        low = level - high - mid
        flag = jnp.where(used, 1.0, 0.0)
        stats = [high, mid, low, flag]
        table = jnp.concatenate(
            [v[:, g * tokens : (g + 1) * tokens] for v in stats for g in range(groups)]
            + [jnp.zeros((hd - 4 * groups, tokens), F32)],
            axis=0,
        )
        outs[i][:, groups * hd :] = table.T.astype(BF16)
        for g in range(groups):
            block = done[:, g * tokens : (g + 1) * tokens]
            outs[i][:, g * hd : (g + 1) * hd] = block.T.astype(BF16)


def flash(seg, pos, qs, spare, kvs, state, last):
    nq, nk = len(qs), len(kvs)
    tokens, width = qs[0].shape
    hd, span = kvs[0].shape[0] // 2, kvs[0].shape[1]
    groups = width // hd
    rows = groups * tokens
    scale2 = math.log2(math.e) * hd ** (-0.5)
    first = state is None
    state_types = [
        jax.ShapeDtypeStruct((8, rows), F32),
        jax.ShapeDtypeStruct((8, rows), F32),
        jax.ShapeDtypeStruct((hd, rows), F32),
    ]
    scratch = [
        pltpu.VMEM((nq, tokens, width), BF16),
        pltpu.VMEM((nq, rows, hd), BF16),
        pltpu.VMEM((nk, 2 * hd, span), BF16),
        pltpu.VMEM((nq, 8, rows), jnp.int32),
        pltpu.VMEM((hd, rows), F32),
        pltpu.SMEM((nq,), jnp.int32),
        pltpu.SMEM((1,), jnp.int32),
    ]
    scratch += [pltpu.VMEM((nq, *t.shape), t.dtype) for t in state_types]
    if last:
        outs = [jax.ShapeDtypeStruct((tokens, width + hd), BF16)] * nq
    else:
        outs = state_types * nq
    scratch += [
        pltpu.SemaphoreType.DMA((nq,)),
        pltpu.SemaphoreType.DMA((nk,)),
        pltpu.SemaphoreType.DMA((3 * nq,)),
        pltpu.VMEM(seg.shape, seg.dtype),
        pltpu.VMEM(pos.shape, pos.dtype),
        pltpu.SemaphoreType.DMA((2,)),
    ]
    return pl.pallas_call(
        functools.partial(flash_kernel, nq, nk, first, last, groups, rows, scale2),
        out_shape=outs,
        in_specs=[ANY] * (3 + nq + nk + (0 if first else 3 * nq)),
        out_specs=[VMEM if last else ANY] * len(outs),
        scratch_shapes=scratch,
        compiler_params=pltpu.CompilerParams(vmem_limit_bytes=FLASH_LIMIT),
        cost_estimate=cost(1e6, 1e5),
    )(seg, pos, *qs, spare, *kvs, *(() if first else state))


def combine_kernel(groups, *refs):
    parts, out = refs[:-1], refs[-1]
    tokens, width = out.shape
    hd = width // groups
    stats = [r[:, width:].astype(F32) for r in parts]
    for g in range(groups):
        levels = []
        for s in stats:
            level = (
                s[:, g : g + 1]
                + s[:, groups + g : groups + g + 1]
                + s[:, 2 * groups + g : 2 * groups + g + 1]
            )
            levels.append(jnp.where(s[:, 3 * groups + g : 3 * groups + g + 1] > 0.0, level, FLOOR))
        top = functools.reduce(jnp.maximum, levels)
        shares = [jnp.where(x > FLOOR, jnp.exp2(x - top), 0.0) for x in levels]
        total = functools.reduce(lambda a, b: a + b, shares)
        summed = 0.0
        for r, share in zip(parts, shares):
            summed = summed + r[:, g * hd : (g + 1) * hd].astype(F32) * share
        out[:, g * hd : (g + 1) * hd] = (summed / total).astype(BF16)


def combine(parts, groups):
    tokens, wide = parts[0].shape
    hd = wide // (groups + 1)
    return pl.pallas_call(
        functools.partial(combine_kernel, groups),
        out_shape=jax.ShapeDtypeStruct((tokens, groups * hd), BF16),
        in_specs=[VMEM] * len(parts),
        out_specs=VMEM,
        compiler_params=pltpu.CompilerParams(vmem_limit_bytes=LIMIT),
        cost_estimate=cost(1e6, 1e6),
    )(*parts)


def project_kernel(nb, nw, *refs):
    ids = refs[0]
    blocks = refs[1 : 1 + nb]
    ws = refs[1 + nb : 1 + nb + nw]
    outs = refs[1 + nb + nw : -1]
    rows_s = refs[-1]
    tokens = blocks[0].shape[0]
    cols = ws[0].shape[1]
    for b in range(nb):
        rows_s[pl.ds(pl.multiple_of(ids[b] * tokens, tokens), tokens), :] = blocks[b][...]
    rows = rows_s[...]
    for w in range(nw):
        y = jnp.dot(rows, ws[w][...], preferred_element_type=F32).astype(BF16)
        for n, out in enumerate(outs):
            for half in range(2):
                lo = (2 * n + half) * tokens
                out[half, :, w * cols : (w + 1) * cols] = y[lo : lo + tokens]


def project(slots, blocks, ws, nx):
    tokens, width = blocks[0].shape
    nb, nw = len(blocks), len(ws)
    cols = ws[0].shape[1]
    out = jax.ShapeDtypeStruct((2, tokens, nw * cols), BF16)
    return pl.pallas_call(
        functools.partial(project_kernel, nb, nw),
        out_shape=[out] * nx,
        in_specs=[SMEM] + [VMEM] * (nb + nw),
        out_specs=[VMEM] * nx,
        scratch_shapes=[pltpu.VMEM((nb * tokens, width), BF16)],
        compiler_params=pltpu.CompilerParams(vmem_limit_bytes=LIMIT),
        cost_estimate=cost(2 * nb * tokens * width * nw * cols, 4e6),
    )(slots, *blocks, *ws)


def swap(array, axis):
    return lax.ppermute(array, axis, [(0, 1), (1, 0)])


def useful(plane, owner):
    return owner >= plane - 1 or plane == NZ - 1


def fetch(array, k, trim):
    pairs = [((z + k) % NZ, z) for z in range(NZ) if not trim or useful(z, (z + k) % NZ)]
    return lax.ppermute(array, "z", pairs)


def give(array, k):
    pairs = [(z, (z + k) % NZ) for z in range(NZ) if useful(z, (z + k) % NZ)]
    return lax.ppermute(array, "z", pairs)


def lender(z, c):
    if c == 0:
        return None if z == LAST - 2 else (z + 1) % NZ
    return {0: None, 1: None, LAST: 0}.get(z, z - 1)


def beside(array):
    pairs = [
        ((lender(z, c) * 2 + y) * 2 + c, (z * 2 + y) * 2 + c)
        for z in range(NZ)
        for y in range(2)
        for c in range(2)
        if lender(z, c) is not None
    ]
    return lax.ppermute(array, ("z", "yh", "core"), pairs)


def per_device(
    queries, latent_keys, latent_values, key_basis, value_basis, out_weight, positions, key_segments
):
    z, yh, core = lax.axis_index("z"), lax.axis_index("yh"), lax.axis_index("core")
    yl, x = lax.axis_index("yl"), lax.axis_index("x")
    tokens, width = queries.shape
    hd = key_basis.shape[2]
    groups = width // hd
    span = latent_keys.shape[0]
    kv = rebuild(latent_keys, latent_values, key_basis, value_basis)
    lent, kv = lax.optimization_barrier((queries, kv))
    q_far = fetch(lent, 4, True)
    q_down = fetch(lent, 6, True)
    spare = lax.ppermute(lent, "z", [(LAST, LAST - 1)])
    qs = [queries, fetch(lent, 2, True), q_down, q_far]
    kv_y = swap(kv, "yh")
    kv_far = beside(kv)

    def both_cores(array):
        return [array, swap(array, "core")]

    seg, pos = key_segments.reshape(-1, 128), positions.reshape(-1, 128)
    kv, kv_y, kv_far, spare, *qs = lax.optimization_barrier((kv, kv_y, kv_far, spare, *qs))
    kv_far_y = swap(kv_far, "yh")
    kvs = both_cores(kv) + both_cores(kv_y) + both_cores(kv_far)
    state = flash(seg, pos, qs, spare, kvs, None, False)
    kv_far_y, out_weight, *state = lax.optimization_barrier((kv_far_y, out_weight, *state))
    w_y = swap(out_weight, "yh")
    parts = flash(seg, pos, qs, spare, both_cores(kv_far_y), state, True)
    back = [parts[0]] + [give(parts[n], SHIFTS[n]) for n in (3, 1, 2)]
    back += [lax.ppermute(parts[1], "z", [(LAST - 1, LAST)])]
    attended = combine(back, groups)
    w_y, attended = lax.optimization_barrier((w_y, attended))
    ws = [out_weight, swap(out_weight, "core"), w_y, swap(w_y, "core")]

    up, down = fetch(attended, 1, False), fetch(attended, NZ - 1, False)
    up2, down2, far = [fetch(attended, k, False) for k in SHIFTS[1:]]
    blocks = [attended, up, down, up2, down2, far, fetch(up2, 1, False), fetch(down2, NZ - 1, False)]
    planes = [(z + k) % NZ for k in (0, 1, 7, 2, 6, 4, 3, 5)]
    slots = [2 * ((p % 4 - x) % 4) + ((p // 4) ^ yl) for p in planes]
    outs = project(jnp.stack(slots).astype(jnp.int32), blocks, ws, 4)

    def along_x(array, k):
        return lax.ppermute(array, "x", [(n, (n + k) % 4) for n in range(4)])

    summed = outs[0].astype(F32)
    for k in (1, 2, 3):
        summed = summed + along_x(outs[k], k).astype(F32)
    half = summed.shape[2] // 2

    def along_y(array, a, b):
        pairs = [(2 * m + n, 2 * (m ^ a) + (n ^ b)) for m in range(2) for n in range(2)]
        return lax.ppermute(array, ("yl", "yh"), pairs)

    sent = summed.astype(BF16)
    from_l = along_y(sent[1, :, :half], 1, 0)
    from_h = along_y(sent[0, :, half:], 0, 1)
    from_lh = along_y(sent[1, :, half:], 1, 1)
    mine = (summed[0, :, :half] + from_l.astype(F32)).astype(BF16)
    theirs = (from_h.astype(F32) + from_lh.astype(F32)).astype(BF16)
    both = jnp.stack([jnp.where(yh == 0, mine, theirs), jnp.where(yh == 0, theirs, mine)])
    cols = half // 2
    here = both[:, :, :cols]
    there = swap(both[:, :, cols:], "core")
    rows = jnp.stack([jnp.where(core == 0, here, there), jnp.where(core == 0, there, here)], axis=1)
    return rows.reshape(-1, cols)


def solution(mesh):
    fine = Mesh(mesh.devices.reshape(2, 4, NZ, 2, 2), ("yl", "x", "z", "yh", "core"))
    head, ctx = ("yl", "x"), ("z", "yh", "core")
    placed = (
        P(ctx, head),
        P(ctx, head),
        P(ctx, head),
        P(head, None, None),
        P(head, None, None),
        P(head, ctx),
        P(),
        P(),
    )
    return jax.shard_map(
        per_device, mesh=fine, in_specs=placed, out_specs=P(head, ctx), check_vma=False
    )
```

profile of v0, /device:TPU:1, one launch (start us, length us, event | category | flops | bytes accessed | tf_op | source)
XLA Modules:
  0.0 156.8 jit_solution(14366436013157047369)
XLA Ops:
  0.0 2.2 %shard_map.82.refs_7_ = bf16[256,1024]{1,0:T(8,128)(2,1)} custom-call(bf16[1024,128]{1,0:T(8,128)(2,1)} %lk_in.1, bf16[1024,128]{1,0:T(8,128)(2,1)} %lv_in.1, bf16[1,128,128]{2,1,0:T(8,128)(2,1)} %bk_in.1, bf16[1,128,128]{2,1,0:T(8,128)(2,1)} %bv_in.1), custom_call_target="tpu_custom_call" | custom-call | flops 67108864 | bytes 1048576 | tf_op jit(solution)/shard_map/pallas_call | solution.py:54
  2.2 3.8 %collective-permute-start = (bf16[256,1024]{1,0:T(8,128)(2,1)}, bf16[256,1024]{1,0:T(8,128)(2,1)S(1)}, u32[]{:S(2)}, u32[]{:S(2)}) collective-permute-start(bf16[256,1024]{1,0:T(8,128)(2,1)} %shard_map.82.refs_7_), channel_id=1, source_target_pairs={{0,2},{2,0},{1,3},{3,1},{4,6},{6,4},{5,7},{7,5},{8,10},{10,8},{9,1... | collective-permute-start | bytes 1572872 | tf_op jit(solution)/shard_map/ppermute | solution.py:401
  6.1 7.5 %collective-permute-start.1 = (bf16[256,1024]{1,0:T(8,128)(2,1)}, bf16[256,1024]{1,0:T(8,128)(2,1)S(1)}, u32[]{:S(2)}, u32[]{:S(2)}) collective-permute-start(bf16[256,1024]{1,0:T(8,128)(2,1)} %shard_map.82.refs_7_), channel_id=1, source_target_pairs={{4,0},{6,2},{8,4},{10,6},{12,8},{5,9},{14,10},{7,11},{16,12},{9,13... | collective-permute-start | bytes 1572872 | tf_op jit(solution)/shard_map/ppermute | solution.py:432
  13.6 0.7 collective-permute-start.2
  14.3 1.3 collective-permute-start.3
  15.6 1.3 collective-permute-start.4
  16.9 1.3 collective-permute-start.5
  18.2 3.6 %collective-permute-done.3.refs_3_ = bf16[64,1024]{1,0:T(8,128)(2,1)S(1)} collective-permute-done((bf16[64,1024]{1,0:T(8,128)(2,1)S(1)}, bf16[64,1024]{1,0:T(8,128)(2,1)S(1)}, u32[]{:S(2)}, u32[]{:S(2)}) %collective-permute-start.3) | collective-permute-done | bytes 131104 | tf_op jit(solution)/shard_map/ppermute | solution.py:410
  21.8 3.6 %collective-permute-done.4.refs_4_ = bf16[64,1024]{1,0:T(8,128)(2,1)S(1)} collective-permute-done((bf16[64,1024]{1,0:T(8,128)(2,1)S(1)}, bf16[64,1024]{1,0:T(8,128)(2,1)S(1)}, u32[]{:S(2)}, u32[]{:S(2)}) %collective-permute-start.4) | collective-permute-done | bytes 131104 | tf_op jit(solution)/shard_map/ppermute | solution.py:410
  25.3 1.4 collective-permute-done.5.refs_5_
  26.7 0.2 collective-permute-done.1.refs_11_
  26.9 5.5 %collective-permute-start.9 = (bf16[256,1024]{1,0:T(8,128)(2,1)S(1)}, bf16[256,1024]{1,0:T(8,128)(2,1)S(1)}, u32[]{:S(2)}, u32[]{:S(2)}) collective-permute-start(bf16[256,1024]{1,0:T(8,128)(2,1)S(1)} %collective-permute-done.1.refs_11_), channel_id=1, source_target_pairs={{0,1},{1,0},{2,3},{3,2},{4,5},{5,4},{6,7},{7,6},{8,9},{9,8},{10,11... | collective-permute-start | bytes 1572872 | tf_op jit(solution)/shard_map/ppermute | solution.py:401
  32.5 0.4 collective-permute-start.8
  33.0 1.0 collective-permute-done.9.refs_12_
  34.0 1.7 %collective-permute-done.7.refs_8_ = bf16[256,1024]{1,0:T(8,128)(2,1)S(1)} collective-permute-done((bf16[256,1024]{1,0:T(8,128)(2,1)}, bf16[256,1024]{1,0:T(8,128)(2,1)S(1)}, u32[]{:S(2)}, u32[]{:S(2)}) %collective-permute-start.7) | collective-permute-done | bytes 524320 | tf_op jit(solution)/shard_map/ppermute | solution.py:401
  35.7 1.0 copy-done
  36.7 10.5 %shard_map.83 = (f32[8,512]{1,0:T(8,128)S(1)}, f32[8,512]{1,0:T(8,128)S(1)}, f32[128,512]{1,0:T(8,128)S(1)}, f32[8,512]{1,0:T(8,128)S(1)}, f32[8,512]{1,0:T(8,12...) custom-call(s32[256,128]{1,0:T(8,128)S(1)} %bitcast.35, ...), custom_call_target="tpu_custom_call" | custom-call | flops 1000000 | bytes 100000 | tf_op jit(solution)/shard_map/pallas_call | solution.py:318
  47.3 0.7 collective-permute-done.6.refs_7_
  47.9 4.1 %collective-permute-start.11 = (bf16[256,1024]{1,0:T(8,128)(2,1)S(1)}, bf16[256,1024]{1,0:T(8,128)(2,1)S(1)}, u32[]{:S(2)}, u32[]{:S(2)}) collective-permute-start(bf16[256,1024]{1,0:T(8,128)(2,1)S(1)} %collective-permute-done.6.refs_7_), channel_id=1, source_target_pairs={{0,1},{1,0},{2,3},{3,2},{4,5},{5,4},{6,7},{7,6},{8,9},{9,8},{10,11... | collective-permute-start | bytes 1572872 | tf_op jit(solution)/shard_map/ppermute | solution.py:401
  52.0 1.5 collective-permute-done.11.refs_8_
  53.6 3.7 %shard_map.84 = (bf16[64,1152]{1,0:T(8,128)(2,1)S(1)}, bf16[64,1152]{1,0:T(8,128)(2,1)S(1)}, bf16[64,1152]{1,0:T(8,128)(2,1)S(1)}, bf16[64,1152]{1,0:T(8,128)(2,1)S(1)}) custom-call(s32[256,128]{1,0:T(8,128)S(1)} %bitcast.36, s32[16,128]{1,0:T(8,128)S(1)} %bitcast.38, bf16[64,1024]{1,0:T(8,128)(2,1)S(1)} %copy-done.2, ...), custom_call_target="tpu_custom_call" | custom-call | flops 1000000 | bytes 100000 | tf_op jit(solution)/shard_map/pallas_call | solution.py:318
  57.2 6.7 %collective-permute-start.12 = (bf16[64,1152]{1,0:T(8,128)(2,1)S(1)}, bf16[64,1152]{1,0:T(8,128)(2,1)S(1)}, u32[]{:S(2)}, u32[]{:S(2)}) collective-permute-start(bf16[64,1152]{1,0:T(8,128)(2,1)S(1)} %get-tuple-element.88), channel_id=1, source_target_pairs={{0,16},{4,20},{8,24},{12,28},{28,12},{1,17},{5,21},{9,25},{13,29},... | collective-permute-start | bytes 442376 | tf_op jit(solution)/shard_map/ppermute | solution.py:415
  63.9 6.0 %collective-permute-start.13 = (bf16[64,1152]{1,0:T(8,128)(2,1)S(1)}, bf16[64,1152]{1,0:T(8,128)(2,1)S(1)}, u32[]{:S(2)}, u32[]{:S(2)}) collective-permute-start(bf16[64,1152]{1,0:T(8,128)(2,1)S(1)} %get-tuple-element.89), channel_id=1, source_target_pairs={{0,8},{4,12},{8,16},{12,20},{16,24},{20,28},{28,4},{1,9},{5,13},{9... | collective-permute-start | bytes 442376 | tf_op jit(solution)/shard_map/ppermute | solution.py:415
  69.9 1.3 collective-permute-start.14
  71.2 0.7 collective-permute-start.15
  71.9 0.7 collective-permute-start.23
  72.7 1.3 collective-permute-done.14.refs_3_
  74.0 0.7 shard_map.85.refs_1_
  74.8 1.3 collective-permute-start.24
  76.1 30.4 %collective-permute-start.18 = (bf16[64,1024]{1,0:T(8,128)(2,1)S(1)}, bf16[64,1024]{1,0:T(8,128)(2,1)S(1)}, u32[]{:S(2)}, u32[]{:S(2)}) collective-permute-start(bf16[64,1024]{1,0:T(8,128)(2,1)S(1)} %shard_map.85.refs_1_), channel_id=1, source_target_pairs={{8,0},{12,4},{16,8},{20,12},{24,16},{28,20},{0,24},{4,28},{9,1},{1... | collective-permute-start | bytes 393224 | tf_op jit(solution)/shard_map/ppermute | solution.py:410
  106.5 4.6 %collective-permute-start.16 = (bf16[64,1024]{1,0:T(8,128)(2,1)S(1)}, bf16[64,1024]{1,0:T(8,128)(2,1)S(1)}, u32[]{:S(2)}, u32[]{:S(2)}) collective-permute-start(bf16[64,1024]{1,0:T(8,128)(2,1)S(1)} %shard_map.85.refs_1_), channel_id=1, source_target_pairs={{4,0},{8,4},{12,8},{16,12},{20,16},{24,20},{28,24},{0,28},{5,1},{9... | collective-permute-start | bytes 393224 | tf_op jit(solution)/shard_map/ppermute | solution.py:410
  111.1 2.7 %collective-permute-start.20 = (bf16[64,1024]{1,0:T(8,128)(2,1)S(1)}, bf16[64,1024]{1,0:T(8,128)(2,1)S(1)}, u32[]{:S(2)}, u32[]{:S(2)}) collective-permute-start(bf16[64,1024]{1,0:T(8,128)(2,1)S(1)} %shard_map.85.refs_1_), channel_id=1, source_target_pairs={{16,0},{20,4},{24,8},{28,12},{0,16},{4,20},{8,24},{12,28},{17,1},{... | collective-permute-start | bytes 393224 | tf_op jit(solution)/shard_map/ppermute | solution.py:410
  113.7 2.5 %collective-permute-done.19.refs_5_ = bf16[64,1024]{1,0:T(8,128)(2,1)S(1)} collective-permute-done((bf16[64,1024]{1,0:T(8,128)(2,1)S(1)}, bf16[64,1024]{1,0:T(8,128)(2,1)S(1)}, u32[]{:S(2)}, u32[]{:S(2)}) %collective-permute-start.19) | collective-permute-done | bytes 131104 | tf_op jit(solution)/shard_map/ppermute | solution.py:410
  116.2 2.0 %collective-permute-start.22 = (bf16[64,1024]{1,0:T(8,128)(2,1)S(1)}, bf16[64,1024]{1,0:T(8,128)(2,1)S(1)}, u32[]{:S(2)}, u32[]{:S(2)}) collective-permute-start(bf16[64,1024]{1,0:T(8,128)(2,1)S(1)} %collective-permute-done.19.refs_5_), channel_id=1, source_target_pairs={{28,0},{0,4},{4,8},{8,12},{12,16},{16,20},{20,24},{24,28},{29,1},{... | collective-permute-start | bytes 393224 | tf_op jit(solution)/shard_map/ppermute | solution.py:410
  118.2 7.2 %collective-permute-done.17.refs_3_ = bf16[64,1024]{1,0:T(8,128)(2,1)S(1)} collective-permute-done((bf16[64,1024]{1,0:T(8,128)(2,1)S(1)}, bf16[64,1024]{1,0:T(8,128)(2,1)S(1)}, u32[]{:S(2)}, u32[]{:S(2)}) %collective-permute-start.17) | collective-permute-done | bytes 131104 | tf_op jit(solution)/shard_map/ppermute | solution.py:410
  125.4 2.8 %collective-permute-done.22.refs_8_ = bf16[64,1024]{1,0:T(8,128)(2,1)S(1)} collective-permute-done((bf16[64,1024]{1,0:T(8,128)(2,1)S(1)}, bf16[64,1024]{1,0:T(8,128)(2,1)S(1)}, u32[]{:S(2)}, u32[]{:S(2)}) %collective-permute-start.22) | collective-permute-done | bytes 131104 | tf_op jit(solution)/shard_map/ppermute | solution.py:410
  128.2 1.9 %shard_map.86 = (bf16[2,64,1024]{2,1,0:T(8,128)(2,1)S(1)}, bf16[2,64,1024]{2,1,0:T(8,128)(2,1)S(1)}, bf16[2,64,1024]{2,1,0:T(8,128)(2,1)S(1)}, bf16[2,64,1024]{2,1,0:T(8,128)(2,1)S(1)}) custom-call(s32[8]{0:T(128)S(1)} %stack.53.refs_0_, bf16[64,1024]{1,0:T(8,128)(2,1)S(1)} %shard_map.85.refs_1_, bf16[64,1024]{1,0:T(8,128)(2,1)S(1)} %collective-permute-done.16.refs_2_, ...), custom_call_target="tpu_custom_call" | custom-call | flops 1073741824 | bytes 4000000 | tf_op jit(solution)/shard_map/pallas_call | solution.py:389
  130.1 1.3 collective-permute-start.25
  131.3 3.7 %collective-permute-start.26 = (bf16[2,64,1024]{2,1,0:T(8,128)(2,1)S(1)}, bf16[2,64,1024]{2,1,0:T(8,128)(2,1)S(1)}, u32[]{:S(2)}, u32[]{:S(2)}) collective-permute-start(bf16[2,64,1024]{2,1,0:T(8,128)(2,1)S(1)} %get-tuple-element.95), channel_id=1, source_target_pairs={{0,64},{32,96},{64,0},{96,32},{1,65},{33,97},{65,1},{97,33},{2,66}... | collective-permute-start | bytes 786440 | tf_op jit(solution)/shard_map/ppermute | solution.py:478
  135.0 2.0 %collective-permute-start.27 = (bf16[2,64,1024]{2,1,0:T(8,128)(2,1)S(1)}, bf16[2,64,1024]{2,1,0:T(8,128)(2,1)S(1)}, u32[]{:S(2)}, u32[]{:S(2)}) collective-permute-start(bf16[2,64,1024]{2,1,0:T(8,128)(2,1)S(1)} %get-tuple-element.96), channel_id=1, source_target_pairs={{0,96},{32,0},{64,32},{96,64},{1,97},{33,1},{65,33},{97,65},{2,98}... | collective-permute-start | bytes 786440 | tf_op jit(solution)/shard_map/ppermute | solution.py:478
  137.0 0.9 collective-permute-done.25
  137.9 8.0 %collective-permute-done.26 = bf16[2,64,1024]{2,1,0:T(8,128)(2,1)S(1)} collective-permute-done((bf16[2,64,1024]{2,1,0:T(8,128)(2,1)S(1)}, bf16[2,64,1024]{2,1,0:T(8,128)(2,1)S(1)}, u32[]{:S(2)}, u32[]{:S(2)}) %collective-permute-start.26) | collective-permute-done | bytes 262176 | tf_op jit(solution)/shard_map/ppermute | solution.py:478
  146.3 3.7 %collective-permute-start.30 = (bf16[64,512]{1,0:T(8,128)(2,1)S(1)}, bf16[64,512]{1,0:T(8,128)(2,1)S(1)}, u32[]{:S(2)}, u32[]{:S(2)}) collective-permute-start(bf16[64,512]{1,0:T(8,128)(2,1)S(1)} %get-tuple-element.102), channel_id=1, source_target_pairs={{0,130},{2,128},{128,2},{130,0},{1,131},{3,129},{129,3},{131,1},{4... | collective-permute-start | bytes 196616 | tf_op jit(solution)/shard_map/ppermute | solution.py:487
  150.1 0.9 collective-permute-done.29
  150.9 0.8 collective-permute-done.30
  151.8 3.4 %collective-permute-start.31 = (bf16[2,64,256]{2,1,0:T(8,128)(2,1)S(1)}, bf16[2,64,256]{2,1,0:T(8,128)(2,1)S(1)}, u32[]{:S(2)}, u32[]{:S(2)}) collective-permute-start(bf16[2,64,256]{2,1,0:T(8,128)(2,1)S(1)} %pad_maximum_fusion.1), channel_id=1, source_target_pairs={{0,1},{1,0},{2,3},{3,2},{4,5},{5,4},{6,7},{7,6},{8,9},{9,8},{10,11... | collective-permute-start | bytes 196616 | tf_op jit(solution)/shard_map/ppermute | solution.py:401
  155.2 0.9 collective-permute-done.31
  156.1 0.7 copy.9
  (39 shorter events, 0.9 us)
Async XLA Ops:
  0.0 13.6 %copy-start.2 = (bf16[64,1024]{1,0:T(8,128)(2,1)S(1)}, bf16[64,1024]{1,0:T(8,128)(2,1)}, u32[]{:S(2)}) copy-start(bf16[64,1024]{1,0:T(8,128)(2,1)} %refs_2_.1) | copy-start | bytes 393220
  0.0 35.7 %copy-start.1 = (s32[32768]{0:T(1024)S(1)}, s32[32768]{0:T(1024)}, u32[]{:S(2)}) copy-start(s32[32768]{0:T(1024)} %param.15) | copy-start | bytes 393220
  0.0 35.7 %copy-start.3 = (s32[2048]{0:T(1024)S(1)}, s32[2048]{0:T(1024)}, u32[]{:S(2)}) copy-start(s32[2048]{0:T(1024)} %param.14) | copy-start | bytes 24580
  2.2 24.5 %collective-permute-start = (bf16[256,1024]{1,0:T(8,128)(2,1)}, bf16[256,1024]{1,0:T(8,128)(2,1)S(1)}, u32[]{:S(2)}, u32[]{:S(2)}) collective-permute-start(bf16[256,1024]{1,0:T(8,128)(2,1)} %shard_map.82.refs_7_), channel_id=1, source_target_pairs={{0,2},{2,0},{1,3},{3,1},{4,6},{6,4},{5,7},{7,5},{8,10},{10,8},{9,1... | collective-permute-start | bytes 1572872 | tf_op jit(solution)/shard_map/ppermute | solution.py:401
  6.1 20.9 %collective-permute-start.1 = (bf16[256,1024]{1,0:T(8,128)(2,1)}, bf16[256,1024]{1,0:T(8,128)(2,1)S(1)}, u32[]{:S(2)}, u32[]{:S(2)}) collective-permute-start(bf16[256,1024]{1,0:T(8,128)(2,1)} %shard_map.82.refs_7_), channel_id=1, source_target_pairs={{4,0},{6,2},{8,4},{10,6},{12,8},{5,9},{14,10},{7,11},{16,12},{9,13... | collective-permute-start | bytes 1572872 | tf_op jit(solution)/shard_map/ppermute | solution.py:432
  13.6 3.3 %collective-permute-start.2 = (bf16[64,1024]{1,0:T(8,128)(2,1)S(1)}, bf16[64,1024]{1,0:T(8,128)(2,1)S(1)}, u32[]{:S(2)}, u32[]{:S(2)}) collective-permute-start(bf16[64,1024]{1,0:T(8,128)(2,1)S(1)} %copy-done.2), channel_id=1, source_target_pairs={{28,24},{29,25},{30,26},{31,27},{60,56},{61,57},{62,58},{63,59},{9... | collective-permute-start | bytes 393224 | tf_op jit(solution)/shard_map/ppermute | solution.py:448
  14.3 7.5 %collective-permute-start.3 = (bf16[64,1024]{1,0:T(8,128)(2,1)S(1)}, bf16[64,1024]{1,0:T(8,128)(2,1)S(1)}, u32[]{:S(2)}, u32[]{:S(2)}) collective-permute-start(bf16[64,1024]{1,0:T(8,128)(2,1)S(1)} %copy-done.2), channel_id=1, source_target_pairs={{8,0},{12,4},{16,8},{20,12},{24,16},{28,20},{4,28},{9,1},{13,5},{1... | collective-permute-start | bytes 393224 | tf_op jit(solution)/shard_map/ppermute | solution.py:410
  15.6 9.8 %collective-permute-start.4 = (bf16[64,1024]{1,0:T(8,128)(2,1)S(1)}, bf16[64,1024]{1,0:T(8,128)(2,1)S(1)}, u32[]{:S(2)}, u32[]{:S(2)}) collective-permute-start(bf16[64,1024]{1,0:T(8,128)(2,1)S(1)} %copy-done.2), channel_id=1, source_target_pairs={{24,0},{28,4},{20,28},{25,1},{29,5},{21,29},{26,2},{30,6},{22,30},... | collective-permute-start | bytes 393224 | tf_op jit(solution)/shard_map/ppermute | solution.py:410
  16.9 9.8 %collective-permute-start.5 = (bf16[64,1024]{1,0:T(8,128)(2,1)S(1)}, bf16[64,1024]{1,0:T(8,128)(2,1)S(1)}, u32[]{:S(2)}, u32[]{:S(2)}) collective-permute-start(bf16[64,1024]{1,0:T(8,128)(2,1)S(1)} %copy-done.2), channel_id=1, source_target_pairs={{16,0},{20,4},{24,8},{28,12},{12,28},{17,1},{21,5},{25,9},{29,13},... | collective-permute-start | bytes 393224 | tf_op jit(solution)/shard_map/ppermute | solution.py:410
  26.9 7.0 %collective-permute-start.9 = (bf16[256,1024]{1,0:T(8,128)(2,1)S(1)}, bf16[256,1024]{1,0:T(8,128)(2,1)S(1)}, u32[]{:S(2)}, u32[]{:S(2)}) collective-permute-start(bf16[256,1024]{1,0:T(8,128)(2,1)S(1)} %collective-permute-done.1.refs_11_), channel_id=1, source_target_pairs={{0,1},{1,0},{2,3},{3,2},{4,5},{5,4},{6,7},{7,6},{8,9},{9,8},{10,11... | collective-permute-start | bytes 1572872 | tf_op jit(solution)/shard_map/ppermute | solution.py:401
  32.4 3.2 %collective-permute-start.7 = (bf16[256,1024]{1,0:T(8,128)(2,1)}, bf16[256,1024]{1,0:T(8,128)(2,1)S(1)}, u32[]{:S(2)}, u32[]{:S(2)}) collective-permute-start(bf16[256,1024]{1,0:T(8,128)(2,1)} %shard_map.82.refs_7_), channel_id=1, source_target_pairs={{0,1},{1,0},{2,3},{3,2},{4,5},{5,4},{6,7},{7,6},{8,9},{9,8},{10,11... | collective-permute-start | bytes 1572872 | tf_op jit(solution)/shard_map/ppermute | solution.py:401
  32.5 3.1 %collective-permute-start.8 = (bf16[256,1024]{1,0:T(8,128)(2,1)S(1)}, bf16[256,1024]{1,0:T(8,128)(2,1)S(1)}, u32[]{:S(2)}, u32[]{:S(2)}) collective-permute-start(bf16[256,1024]{1,0:T(8,128)(2,1)S(1)} %collective-permute-done.refs_9_), channel_id=1, source_target_pairs={{0,1},{1,0},{2,3},{3,2},{4,5},{5,4},{6,7},{7,6},{8,9},{9,8},{10,11... | collective-permute-start | bytes 1572872 | tf_op jit(solution)/shard_map/ppermute | solution.py:401
  32.9 15.0 %collective-permute-start.6 = (bf16[256,1024]{1,0:T(8,128)(2,1)S(1)}, bf16[256,1024]{1,0:T(8,128)(2,1)S(1)}, u32[]{:S(2)}, u32[]{:S(2)}) collective-permute-start(bf16[256,1024]{1,0:T(8,128)(2,1)S(1)} %collective-permute-done.1.refs_11_), channel_id=1, source_target_pairs={{0,2},{2,0},{1,3},{3,1},{4,6},{6,4},{5,7},{7,5},{8,10},{10,8},{9,1... | collective-permute-start | bytes 1572872 | tf_op jit(solution)/shard_map/ppermute | solution.py:401
  35.7 1.0 copy-start
  36.7 15.3 %copy-start.4 = (bf16[1024,256]{1,0:T(8,128)(2,1)S(1)}, bf16[1024,256]{1,0:T(8,128)(2,1)}, u32[]{:S(2)}) copy-start(bf16[1024,256]{1,0:T(8,128)(2,1)} %refs_9_) | copy-start | bytes 1572868
  47.9 5.7 %collective-permute-start.11 = (bf16[256,1024]{1,0:T(8,128)(2,1)S(1)}, bf16[256,1024]{1,0:T(8,128)(2,1)S(1)}, u32[]{:S(2)}, u32[]{:S(2)}) collective-permute-start(bf16[256,1024]{1,0:T(8,128)(2,1)S(1)} %collective-permute-done.6.refs_7_), channel_id=1, source_target_pairs={{0,1},{1,0},{2,3},{3,2},{4,5},{5,4},{6,7},{7,6},{8,9},{9,8},{10,11... | collective-permute-start | bytes 1572872 | tf_op jit(solution)/shard_map/ppermute | solution.py:401
  52.0 22.7 %collective-permute-start.10 = (bf16[1024,256]{1,0:T(8,128)(2,1)S(1)}, bf16[1024,256]{1,0:T(8,128)(2,1)S(1)}, u32[]{:S(2)}, u32[]{:S(2)}) collective-permute-start(bf16[1024,256]{1,0:T(8,128)(2,1)S(1)} %copy-done.4), channel_id=1, source_target_pairs={{0,2},{2,0},{1,3},{3,1},{4,6},{6,4},{5,7},{7,5},{8,10},{10,8},{9,1... | collective-permute-start | bytes 1572872 | tf_op jit(solution)/shard_map/ppermute | solution.py:401
  57.2 14.6 %collective-permute-start.12 = (bf16[64,1152]{1,0:T(8,128)(2,1)S(1)}, bf16[64,1152]{1,0:T(8,128)(2,1)S(1)}, u32[]{:S(2)}, u32[]{:S(2)}) collective-permute-start(bf16[64,1152]{1,0:T(8,128)(2,1)S(1)} %get-tuple-element.88), channel_id=1, source_target_pairs={{0,16},{4,20},{8,24},{12,28},{28,12},{1,17},{5,21},{9,25},{13,29},... | collective-permute-start | bytes 442376 | tf_op jit(solution)/shard_map/ppermute | solution.py:415
  63.9 8.8 %collective-permute-start.13 = (bf16[64,1152]{1,0:T(8,128)(2,1)S(1)}, bf16[64,1152]{1,0:T(8,128)(2,1)S(1)}, u32[]{:S(2)}, u32[]{:S(2)}) collective-permute-start(bf16[64,1152]{1,0:T(8,128)(2,1)S(1)} %get-tuple-element.89), channel_id=1, source_target_pairs={{0,8},{4,12},{8,16},{12,20},{16,24},{20,28},{28,4},{1,9},{5,13},{9... | collective-permute-start | bytes 442376 | tf_op jit(solution)/shard_map/ppermute | solution.py:415
  69.9 4.2 %collective-permute-start.14 = (bf16[64,1152]{1,0:T(8,128)(2,1)S(1)}, bf16[64,1152]{1,0:T(8,128)(2,1)S(1)}, u32[]{:S(2)}, u32[]{:S(2)}) collective-permute-start(bf16[64,1152]{1,0:T(8,128)(2,1)S(1)} %get-tuple-element.90), channel_id=1, source_target_pairs={{0,24},{4,28},{28,20},{1,25},{5,29},{29,21},{2,26},{6,30},{30,22},... | collective-permute-start | bytes 442376 | tf_op jit(solution)/shard_map/ppermute | solution.py:415
  71.2 2.8 %collective-permute-start.15 = (bf16[64,1152]{1,0:T(8,128)(2,1)S(1)}, bf16[64,1152]{1,0:T(8,128)(2,1)S(1)}, u32[]{:S(2)}, u32[]{:S(2)}) collective-permute-start(bf16[64,1152]{1,0:T(8,128)(2,1)S(1)} %get-tuple-element.89), channel_id=1, source_target_pairs={{24,28},{25,29},{26,30},{27,31},{56,60},{57,61},{58,62},{59,63},{8... | collective-permute-start | bytes 442376 | tf_op jit(solution)/shard_map/ppermute | solution.py:465
  71.9 39.2 %collective-permute-start.23 = (bf16[1024,256]{1,0:T(8,128)(2,1)S(1)}, bf16[1024,256]{1,0:T(8,128)(2,1)S(1)}, u32[]{:S(2)}, u32[]{:S(2)}) collective-permute-start(bf16[1024,256]{1,0:T(8,128)(2,1)S(1)} %copy-done.4), channel_id=1, source_target_pairs={{0,1},{1,0},{2,3},{3,2},{4,5},{5,4},{6,7},{7,6},{8,9},{9,8},{10,11... | collective-permute-start | bytes 1572872 | tf_op jit(solution)/shard_map/ppermute | solution.py:401
  74.8 53.4 %collective-permute-start.24 = (bf16[1024,256]{1,0:T(8,128)(2,1)S(1)}, bf16[1024,256]{1,0:T(8,128)(2,1)S(1)}, u32[]{:S(2)}, u32[]{:S(2)}) collective-permute-start(bf16[1024,256]{1,0:T(8,128)(2,1)S(1)} %collective-permute-done.10.refs_11_), channel_id=1, source_target_pairs={{0,1},{1,0},{2,3},{3,2},{4,5},{5,4},{6,7},{7,6},{8,9},{9,8},{10,11... | collective-permute-start | bytes 1572872 | tf_op jit(solution)/shard_map/ppermute | solution.py:401
  76.1 35.0 %collective-permute-start.18 = (bf16[64,1024]{1,0:T(8,128)(2,1)S(1)}, bf16[64,1024]{1,0:T(8,128)(2,1)S(1)}, u32[]{:S(2)}, u32[]{:S(2)}) collective-permute-start(bf16[64,1024]{1,0:T(8,128)(2,1)S(1)} %shard_map.85.refs_1_), channel_id=1, source_target_pairs={{8,0},{12,4},{16,8},{20,12},{24,16},{28,20},{0,24},{4,28},{9,1},{1... | collective-permute-start | bytes 393224 | tf_op jit(solution)/shard_map/ppermute | solution.py:410
  106.5 9.7 %collective-permute-start.19 = (bf16[64,1024]{1,0:T(8,128)(2,1)S(1)}, bf16[64,1024]{1,0:T(8,128)(2,1)S(1)}, u32[]{:S(2)}, u32[]{:S(2)}) collective-permute-start(bf16[64,1024]{1,0:T(8,128)(2,1)S(1)} %shard_map.85.refs_1_), channel_id=1, source_target_pairs={{24,0},{28,4},{0,8},{4,12},{8,16},{12,20},{16,24},{20,28},{25,1},{... | collective-permute-start | bytes 393224 | tf_op jit(solution)/shard_map/ppermute | solution.py:410
  106.5 9.7 %collective-permute-start.16 = (bf16[64,1024]{1,0:T(8,128)(2,1)S(1)}, bf16[64,1024]{1,0:T(8,128)(2,1)S(1)}, u32[]{:S(2)}, u32[]{:S(2)}) collective-permute-start(bf16[64,1024]{1,0:T(8,128)(2,1)S(1)} %shard_map.85.refs_1_), channel_id=1, source_target_pairs={{4,0},{8,4},{12,8},{16,12},{20,16},{24,20},{28,24},{0,28},{5,1},{9... | collective-permute-start | bytes 393224 | tf_op jit(solution)/shard_map/ppermute | solution.py:410
  111.1 14.3 %collective-permute-start.17 = (bf16[64,1024]{1,0:T(8,128)(2,1)S(1)}, bf16[64,1024]{1,0:T(8,128)(2,1)S(1)}, u32[]{:S(2)}, u32[]{:S(2)}) collective-permute-start(bf16[64,1024]{1,0:T(8,128)(2,1)S(1)} %shard_map.85.refs_1_), channel_id=1, source_target_pairs={{28,0},{0,4},{4,8},{8,12},{12,16},{16,20},{20,24},{24,28},{29,1},{... | collective-permute-start | bytes 393224 | tf_op jit(solution)/shard_map/ppermute | solution.py:410
  111.1 14.3 %collective-permute-start.20 = (bf16[64,1024]{1,0:T(8,128)(2,1)S(1)}, bf16[64,1024]{1,0:T(8,128)(2,1)S(1)}, u32[]{:S(2)}, u32[]{:S(2)}) collective-permute-start(bf16[64,1024]{1,0:T(8,128)(2,1)S(1)} %shard_map.85.refs_1_), channel_id=1, source_target_pairs={{16,0},{20,4},{24,8},{28,12},{0,16},{4,20},{8,24},{12,28},{17,1},{... | collective-permute-start | bytes 393224 | tf_op jit(solution)/shard_map/ppermute | solution.py:410
  116.2 9.2 %collective-permute-start.21 = (bf16[64,1024]{1,0:T(8,128)(2,1)S(1)}, bf16[64,1024]{1,0:T(8,128)(2,1)S(1)}, u32[]{:S(2)}, u32[]{:S(2)}) collective-permute-start(bf16[64,1024]{1,0:T(8,128)(2,1)S(1)} %collective-permute-done.18.refs_4_), channel_id=1, source_target_pairs={{4,0},{8,4},{12,8},{16,12},{20,16},{24,20},{28,24},{0,28},{5,1},{9... | collective-permute-start | bytes 393224 | tf_op jit(solution)/shard_map/ppermute | solution.py:410
  116.2 12.0 %collective-permute-start.22 = (bf16[64,1024]{1,0:T(8,128)(2,1)S(1)}, bf16[64,1024]{1,0:T(8,128)(2,1)S(1)}, u32[]{:S(2)}, u32[]{:S(2)}) collective-permute-start(bf16[64,1024]{1,0:T(8,128)(2,1)S(1)} %collective-permute-done.19.refs_5_), channel_id=1, source_target_pairs={{28,0},{0,4},{4,8},{8,12},{12,16},{16,20},{20,24},{24,28},{29,1},{... | collective-permute-start | bytes 393224 | tf_op jit(solution)/shard_map/ppermute | solution.py:410
  130.1 7.8 %collective-permute-start.25 = (bf16[2,64,1024]{2,1,0:T(8,128)(2,1)S(1)}, bf16[2,64,1024]{2,1,0:T(8,128)(2,1)S(1)}, u32[]{:S(2)}, u32[]{:S(2)}) collective-permute-start(bf16[2,64,1024]{2,1,0:T(8,128)(2,1)S(1)} %get-tuple-element.94), channel_id=1, source_target_pairs={{0,32},{32,64},{64,96},{96,0},{1,33},{33,65},{65,97},{97,1},{2,34}... | collective-permute-start | bytes 786440 | tf_op jit(solution)/shard_map/ppermute | solution.py:478
  131.3 14.5 %collective-permute-start.26 = (bf16[2,64,1024]{2,1,0:T(8,128)(2,1)S(1)}, bf16[2,64,1024]{2,1,0:T(8,128)(2,1)S(1)}, u32[]{:S(2)}, u32[]{:S(2)}) collective-permute-start(bf16[2,64,1024]{2,1,0:T(8,128)(2,1)S(1)} %get-tuple-element.95), channel_id=1, source_target_pairs={{0,64},{32,96},{64,0},{96,32},{1,65},{33,97},{65,1},{97,33},{2,66}... | collective-permute-start | bytes 786440 | tf_op jit(solution)/shard_map/ppermute | solution.py:478
  135.0 10.9 %collective-permute-start.27 = (bf16[2,64,1024]{2,1,0:T(8,128)(2,1)S(1)}, bf16[2,64,1024]{2,1,0:T(8,128)(2,1)S(1)}, u32[]{:S(2)}, u32[]{:S(2)}) collective-permute-start(bf16[2,64,1024]{2,1,0:T(8,128)(2,1)S(1)} %get-tuple-element.96), channel_id=1, source_target_pairs={{0,96},{32,0},{64,32},{96,64},{1,97},{33,1},{65,33},{97,65},{2,98}... | collective-permute-start | bytes 786440 | tf_op jit(solution)/shard_map/ppermute | solution.py:478
  146.1 3.9 %collective-permute-start.28 = (bf16[64,512]{1,0:T(8,128)(2,1)S(1)}, bf16[64,512]{1,0:T(8,128)(2,1)S(1)}, u32[]{:S(2)}, u32[]{:S(2)}) collective-permute-start(bf16[64,512]{1,0:T(8,128)(2,1)S(1)} %get-tuple-element.101), channel_id=1, source_target_pairs={{0,128},{2,130},{128,0},{130,2},{1,129},{3,131},{129,1},{131,3},{4... | collective-permute-start | bytes 196616 | tf_op jit(solution)/shard_map/ppermute | solution.py:487
  146.2 4.7 %collective-permute-start.29 = (bf16[64,512]{1,0:T(8,128)(2,1)S(1)}, bf16[64,512]{1,0:T(8,128)(2,1)S(1)}, u32[]{:S(2)}, u32[]{:S(2)}) collective-permute-start(bf16[64,512]{1,0:T(8,128)(2,1)S(1)} %get-tuple-element.103), channel_id=1, source_target_pairs={{0,2},{2,0},{128,130},{130,128},{1,3},{3,1},{129,131},{131,129},{4... | collective-permute-start | bytes 196616 | tf_op jit(solution)/shard_map/ppermute | solution.py:487
  146.3 5.4 %collective-permute-start.30 = (bf16[64,512]{1,0:T(8,128)(2,1)S(1)}, bf16[64,512]{1,0:T(8,128)(2,1)S(1)}, u32[]{:S(2)}, u32[]{:S(2)}) collective-permute-start(bf16[64,512]{1,0:T(8,128)(2,1)S(1)} %get-tuple-element.102), channel_id=1, source_target_pairs={{0,130},{2,128},{128,2},{130,0},{1,131},{3,129},{129,3},{131,1},{4... | collective-permute-start | bytes 196616 | tf_op jit(solution)/shard_map/ppermute | solution.py:487
  151.8 4.3 %collective-permute-start.31 = (bf16[2,64,256]{2,1,0:T(8,128)(2,1)S(1)}, bf16[2,64,256]{2,1,0:T(8,128)(2,1)S(1)}, u32[]{:S(2)}, u32[]{:S(2)}) collective-permute-start(bf16[2,64,256]{2,1,0:T(8,128)(2,1)S(1)} %pad_maximum_fusion.1), channel_id=1, source_target_pairs={{0,1},{1,0},{2,3},{3,2},{4,5},{5,4},{6,7},{7,6},{8,9},{9,8},{10,11... | collective-permute-start | bytes 196616 | tf_op jit(solution)/shard_map/ppermute | solution.py:401
where the time goes:
time: 155 us; the launch traced here: 157 us
  starting transfers between devices  96.6 us (62%)
  waiting for transfers between devices  38.9 us (25%)
  Pallas kernels  19 us (12%)
  local copies, waits for them, and re-layouts  1.82 us (1%)
    ppermute x10, starting transfers between devices, fetch(): return lax.ppermute(array, 'z', pairs)  43.5 us
    ppermute x10, waiting for transfers between devices, fetch(): return lax.ppermute(array, 'z', pairs)  20.9 us
    ppermute x10, starting transfers between devices, swap(): return lax.ppermute(array, axis, [(0, 1), (1, 0)])  19.5 us
    pallas_call x2, Pallas kernels, flash(): pl.pallas_call(functools.partial(flash_kernel, nq, nk, first, last, group...  14.2 us
    ppermute x3, starting transfers between devices, give(): return lax.ppermute(array, 'z', pairs)  13.9 us
    ppermute x3, waiting for transfers between devices, along_x(): return lax.ppermute(array, 'x', [(n, (n + k) % 4) for n in range(4)])  8.89 us
    ppermute x1, starting transfers between devices, beside(): return lax.ppermute(array, ('z', 'yh', 'core'), pairs)  7.5 us
    ppermute x3, starting transfers between devices, along_x(): return lax.ppermute(array, 'x', [(n, (n + k) % 4) for n in range(4)])  6.94 us
  transfers between devices with their start and end apart: 32, of which 18 were waited for; matrix products, arithmetic and copies ran while one was open for 0% of the time, Pallas kernels for 10%

commit v1 on v0

--- a/solution.py
+++ b/solution.py
@@ -79,7 +79,7 @@
     else:
         outs = refs[at : at + 3 * nq]
         at += 3 * nq
-    flat_s, q_s, kv_s, pos_s, acc_t, begun, todo, m_s, l_s, acc_s, *rest = refs[at:]
+    flat_s, q_s, kv_s, pos_s, acc_t, begun, m_s, l_s, acc_s, *rest = refs[at:]
     q_sem, kv_sem, st_sem, seg_ref, pos_ref, small_sem = rest
     hd = kvs[0].shape[0] // 2
     span = kvs[0].shape[1]
@@ -207,13 +207,15 @@
     for i in range(nq):
         begun[i] = (jnp.max(m_s[i]) > 0.5 * FLOOR).astype(jnp.int32) if not first else jnp.int32(0)
 
+    asked = [query_block(n) for n in range(nq)]
+
     def one(n, carry):
-        j = n // nq
-        i = n % nq
+        j = lax.div(n, jnp.int32(nq))
+        i = lax.rem(n, jnp.int32(nq))
         ck = key_block(j)
-        cq = query_block(0)
-        for n in range(1, nq):
-            cq = jnp.where(i == n, query_block(n), cq)
+        cq = asked[0]
+        for m in range(1, nq):
+            cq = jnp.where(i == m, asked[m], cq)
         lent = (i == 1) & (z == LAST - 1)
         cq = jnp.where(lent & (j >= 4 if first else True), -1, cq)
         begin_k, end_k = ck * span, (ck + 1) * span
@@ -221,7 +223,6 @@
         apart = (cut >= end_k) & (cut <= begin_q)
         whole = (ck < cq) & ((cut <= begin_k) | (cut >= end_q))
         some = (ck <= cq) & jnp.logical_not(apart)
-        todo[0] = some.astype(jnp.int32)
 
         @pl.when(i == 0)
         def _():
@@ -235,11 +236,13 @@
             m_s[i] = jnp.broadcast_to(jnp.max(s, axis=0, keepdims=True), (8, rows))
             begun[i] = 1
 
-        @pl.when(whole)
-        def _():
-            todo[0] = 1 - fast_unit(i, j).astype(jnp.int32)
-
-        @pl.when(todo[0] > 0)
+        left = lax.cond(
+            whole,
+            lambda: 1 - fast_unit(i, j).astype(jnp.int32),
+            lambda: some.astype(jnp.int32),
+        )
+
+        @pl.when(left > 0)
         def _():
             safe_unit(i, j, ck)
             begun[i] = 1
@@ -300,7 +303,6 @@
         pltpu.VMEM((nq, 8, rows), jnp.int32),
         pltpu.VMEM((hd, rows), F32),
         pltpu.SMEM((nq,), jnp.int32),
-        pltpu.SMEM((1,), jnp.int32),
     ]
     scratch += [pltpu.VMEM((nq, *t.shape), t.dtype) for t in state_types]
     if last:
@@ -442,7 +444,7 @@
     groups = width // hd
     span = latent_keys.shape[0]
     kv = rebuild(latent_keys, latent_values, key_basis, value_basis)
-    lent, kv = lax.optimization_barrier((queries, kv))
+    lent = queries
     q_far = fetch(lent, 4, True)
     q_down = fetch(lent, 6, True)
     spare = lax.ppermute(lent, "z", [(LAST, LAST - 1)])
@@ -454,7 +456,11 @@
         return [array, swap(array, "core")]
 
     seg, pos = key_segments.reshape(-1, 128), positions.reshape(-1, 128)
-    kv, kv_y, kv_far, spare, *qs = lax.optimization_barrier((kv, kv_y, kv_far, spare, *qs))
+    q_up, q_down, q_far = qs[1:]
+    q_far, q_up, q_down, kv, kv_y, kv_far, spare = lax.optimization_barrier(
+        (q_far, q_up, q_down, kv, kv_y, kv_far, spare)
+    )
+    qs = [queries, q_up, q_down, q_far]
     kv_far_y = swap(kv_far, "yh")
     kvs = both_cores(kv) + both_cores(kv_y) + both_cores(kv_far)
     state = flash(seg, pos, qs, spare, kvs, None, False)

time: 155 us -> 153 us (0.987)
  starting transfers between devices: 96.6 us -> 57.9 us
  Pallas kernels: 19 us -> 42.2 us
  waiting for transfers between devices: 38.9 us -> 51.4 us
    ppermute x10, starting transfers between devices: 43.5 us -> 18.7 us  [fetch(): return lax.ppermute(array, 'z', pairs)]
    pallas_call x2, Pallas kernels: 14.2 us -> 37.4 us  [flash(): pl.pallas_call(functools.partial(flash_kernel, nq, nk, first, last, group...]
    ppermute x10, starting transfers between devices: 19.5 us -> 11.3 us  [swap(): return lax.ppermute(array, axis, [(0, 1), (1, 0)])]
    ppermute x3, starting transfers between devices: 13.9 us -> 7.28 us  [give(): return lax.ppermute(array, 'z', pairs)]
    ppermute x3, waiting for transfers between devices: 1.43 us -> 6.4 us  [give(): return lax.ppermute(array, 'z', pairs)]
    ppermute x10, waiting for transfers between devices: 20.9 us -> 25.2 us  [fetch(): return lax.ppermute(array, 'z', pairs)]
    ppermute x3, waiting for transfers between devices: 1.65 us -> 4.84 us  [along_y(): return lax.ppermute(array, ('yl', 'yh'), pairs)]
  transfers between devices with their start and end apart: 32 -> 32, of which waited for: 18 -> 16; matrix products, arithmetic and copies ran while one was open for 0% -> 0% of each run, Pallas kernels for 10% -> 25%
where the time goes in v1:
time: 153 us; the launch traced here: 154 us
  starting transfers between devices  57.9 us (38%)
  waiting for transfers between devices  51.4 us (34%)
  Pallas kernels  42.2 us (28%)
  local copies, waits for them, and re-layouts  1.82 us (1%)
    pallas_call x2, Pallas kernels, flash(): pl.pallas_call(functools.partial(flash_kernel, nq, nk, first, last, group...  37.4 us
    ppermute x10, waiting for transfers between devices, fetch(): return lax.ppermute(array, 'z', pairs)  25.2 us
    ppermute x10, starting transfers between devices, fetch(): return lax.ppermute(array, 'z', pairs)  18.7 us
    ppermute x10, starting transfers between devices, swap(): return lax.ppermute(array, axis, [(0, 1), (1, 0)])  11.3 us
    ppermute x3, waiting for transfers between devices, along_x(): return lax.ppermute(array, 'x', [(n, (n + k) % 4) for n in range(4)])  9.81 us
    ppermute x1, starting transfers between devices, beside(): return lax.ppermute(array, ('z', 'yh', 'core'), pairs)  7.5 us
    ppermute x3, starting transfers between devices, give(): return lax.ppermute(array, 'z', pairs)  7.28 us
    ppermute x3, starting transfers between devices, along_x(): return lax.ppermute(array, 'x', [(n, (n + k) % 4) for n in range(4)])  6.53 us
  transfers between devices with their start and end apart: 32, of which 16 were waited for; matrix products, arithmetic and copies ran while one was open for 0% of the time, Pallas kernels for 25%

profile of v1, /device:TPU:1, one launch (start us, length us, event | category | flops | bytes accessed | tf_op | source)
XLA Modules:
  0.0 153.7 jit_solution(7195556629355965429)
XLA Ops:
  0.0 2.2 %shard_map.82.refs_7_ = bf16[256,1024]{1,0:T(8,128)(2,1)} custom-call(bf16[1024,128]{1,0:T(8,128)(2,1)} %lk_in.1, bf16[1024,128]{1,0:T(8,128)(2,1)} %lv_in.1, bf16[1,128,128]{2,1,0:T(8,128)(2,1)} %bk_in.1, bf16[1,128,128]{2,1,0:T(8,128)(2,1)} %bv_in.1), custom_call_target="tpu_custom_call" | custom-call | flops 67108864 | bytes 1048576 | tf_op jit(solution)/shard_map/pallas_call | solution.py:54
  2.2 3.8 %collective-permute-start.3 = (bf16[256,1024]{1,0:T(8,128)(2,1)}, bf16[256,1024]{1,0:T(8,128)(2,1)S(1)}, u32[]{:S(2)}, u32[]{:S(2)}) collective-permute-start(bf16[256,1024]{1,0:T(8,128)(2,1)} %shard_map.82.refs_7_), channel_id=1, source_target_pairs={{0,2},{2,0},{1,3},{3,1},{4,6},{6,4},{5,7},{7,5},{8,10},{10,8},{9,1... | collective-permute-start | bytes 1572872 | tf_op jit(solution)/shard_map/ppermute | solution.py:403
  6.1 7.5 %collective-permute-start.4 = (bf16[256,1024]{1,0:T(8,128)(2,1)}, bf16[256,1024]{1,0:T(8,128)(2,1)S(1)}, u32[]{:S(2)}, u32[]{:S(2)}) collective-permute-start(bf16[256,1024]{1,0:T(8,128)(2,1)} %shard_map.82.refs_7_), channel_id=1, source_target_pairs={{4,0},{6,2},{8,4},{10,6},{12,8},{5,9},{14,10},{7,11},{16,12},{9,13... | collective-permute-start | bytes 1572872 | tf_op jit(solution)/shard_map/ppermute | solution.py:434
  13.6 1.3 collective-permute-start
  14.9 1.3 collective-permute-start.1
  16.2 1.3 collective-permute-start.2
  17.5 6.8 %collective-permute-done.refs_5_ = bf16[64,1024]{1,0:T(8,128)(2,1)S(1)} collective-permute-done((bf16[64,1024]{1,0:T(8,128)(2,1)S(1)}, bf16[64,1024]{1,0:T(8,128)(2,1)S(1)}, u32[]{:S(2)}, u32[]{:S(2)}) %collective-permute-start) | collective-permute-done | bytes 131104 | tf_op jit(solution)/shard_map/ppermute | solution.py:412
  24.3 0.7 collective-permute-start.5
  25.0 3.9 %collective-permute-done.1.refs_3_ = bf16[64,1024]{1,0:T(8,128)(2,1)S(1)} collective-permute-done((bf16[64,1024]{1,0:T(8,128)(2,1)S(1)}, bf16[64,1024]{1,0:T(8,128)(2,1)S(1)}, u32[]{:S(2)}, u32[]{:S(2)}) %collective-permute-start.1) | collective-permute-done | bytes 131104 | tf_op jit(solution)/shard_map/ppermute | solution.py:412
  28.9 1.2 collective-permute-done.2.refs_4_
  30.0 1.8 %collective-permute-start.9 = (bf16[256,1024]{1,0:T(8,128)(2,1)S(1)}, bf16[256,1024]{1,0:T(8,128)(2,1)S(1)}, u32[]{:S(2)}, u32[]{:S(2)}) collective-permute-start(bf16[256,1024]{1,0:T(8,128)(2,1)S(1)} %collective-permute-done.4.refs_11_), channel_id=1, source_target_pairs={{0,1},{1,0},{2,3},{3,2},{4,5},{5,4},{6,7},{7,6},{8,9},{9,8},{10,11... | collective-permute-start | bytes 1572872 | tf_op jit(solution)/shard_map/ppermute | solution.py:403
  31.9 0.4 collective-permute-start.8
  32.4 1.0 collective-permute-done.9.refs_12_
  33.4 1.7 %collective-permute-done.7.refs_8_ = bf16[256,1024]{1,0:T(8,128)(2,1)S(1)} collective-permute-done((bf16[256,1024]{1,0:T(8,128)(2,1)}, bf16[256,1024]{1,0:T(8,128)(2,1)S(1)}, u32[]{:S(2)}, u32[]{:S(2)}) %collective-permute-start.7) | collective-permute-done | bytes 524320 | tf_op jit(solution)/shard_map/ppermute | solution.py:403
  35.1 1.0 copy-done
  36.1 31.0 %shard_map.83 = (f32[8,512]{1,0:T(8,128)S(1)}, f32[8,512]{1,0:T(8,128)S(1)}, f32[128,512]{1,0:T(8,128)S(1)}, f32[8,512]{1,0:T(8,128)S(1)}, f32[8,512]{1,0:T(8,12...) custom-call(s32[256,128]{1,0:T(8,128)S(1)} %bitcast.35, ...), custom_call_target="tpu_custom_call" | custom-call | flops 1000000 | bytes 100000 | tf_op jit(solution)/shard_map/pallas_call | solution.py:320
  67.1 2.2 %collective-permute-start.11 = (bf16[256,1024]{1,0:T(8,128)(2,1)S(1)}, bf16[256,1024]{1,0:T(8,128)(2,1)S(1)}, u32[]{:S(2)}, u32[]{:S(2)}) collective-permute-start(bf16[256,1024]{1,0:T(8,128)(2,1)S(1)} %collective-permute-done.6.refs_7_), channel_id=1, source_target_pairs={{0,1},{1,0},{2,3},{3,2},{4,5},{5,4},{6,7},{7,6},{8,9},{9,8},{10,11... | collective-permute-start | bytes 1572872 | tf_op jit(solution)/shard_map/ppermute | solution.py:403
  69.3 1.5 collective-permute-done.11.refs_8_
  70.9 6.4 %shard_map.84 = (bf16[64,1152]{1,0:T(8,128)(2,1)S(1)}, bf16[64,1152]{1,0:T(8,128)(2,1)S(1)}, bf16[64,1152]{1,0:T(8,128)(2,1)S(1)}, bf16[64,1152]{1,0:T(8,128)(2,1)S(1)}) custom-call(s32[256,128]{1,0:T(8,128)S(1)} %bitcast.36, s32[16,128]{1,0:T(8,128)S(1)} %bitcast.38, bf16[64,1024]{1,0:T(8,128)(2,1)S(1)} %copy-done.2, ...), custom_call_target="tpu_custom_call" | custom-call | flops 1000000 | bytes 100000 | tf_op jit(solution)/shard_map/pallas_call | solution.py:320
  77.3 1.3 collective-permute-start.12
  78.6 4.7 %collective-permute-start.13 = (bf16[64,1152]{1,0:T(8,128)(2,1)S(1)}, bf16[64,1152]{1,0:T(8,128)(2,1)S(1)}, u32[]{:S(2)}, u32[]{:S(2)}) collective-permute-start(bf16[64,1152]{1,0:T(8,128)(2,1)S(1)} %get-tuple-element.83), channel_id=1, source_target_pairs={{0,8},{4,12},{8,16},{12,20},{16,24},{20,28},{28,4},{1,9},{5,13},{9... | collective-permute-start | bytes 442376 | tf_op jit(solution)/shard_map/ppermute | solution.py:417
  83.3 1.3 collective-permute-start.14
  84.6 0.7 collective-permute-start.15
  85.4 6.4 %collective-permute-done.14.refs_3_ = bf16[64,1152]{1,0:T(8,128)(2,1)S(1)} collective-permute-done((bf16[64,1152]{1,0:T(8,128)(2,1)S(1)}, bf16[64,1152]{1,0:T(8,128)(2,1)S(1)}, u32[]{:S(2)}, u32[]{:S(2)}) %collective-permute-start.14) | collective-permute-done | bytes 147488 | tf_op jit(solution)/shard_map/ppermute | solution.py:417
  91.8 0.7 shard_map.85.refs_1_
  92.6 7.2 %collective-permute-start.18 = (bf16[64,1024]{1,0:T(8,128)(2,1)S(1)}, bf16[64,1024]{1,0:T(8,128)(2,1)S(1)}, u32[]{:S(2)}, u32[]{:S(2)}) collective-permute-start(bf16[64,1024]{1,0:T(8,128)(2,1)S(1)} %shard_map.85.refs_1_), channel_id=1, source_target_pairs={{8,0},{12,4},{16,8},{20,12},{24,16},{28,20},{0,24},{4,28},{9,1},{1... | collective-permute-start | bytes 393224 | tf_op jit(solution)/shard_map/ppermute | solution.py:412
  99.8 4.6 %collective-permute-start.16 = (bf16[64,1024]{1,0:T(8,128)(2,1)S(1)}, bf16[64,1024]{1,0:T(8,128)(2,1)S(1)}, u32[]{:S(2)}, u32[]{:S(2)}) collective-permute-start(bf16[64,1024]{1,0:T(8,128)(2,1)S(1)} %shard_map.85.refs_1_), channel_id=1, source_target_pairs={{4,0},{8,4},{12,8},{16,12},{20,16},{24,20},{28,24},{0,28},{5,1},{9... | collective-permute-start | bytes 393224 | tf_op jit(solution)/shard_map/ppermute | solution.py:412
  104.4 1.3 collective-permute-start.20
  105.7 3.6 %collective-permute-done.19.refs_5_ = bf16[64,1024]{1,0:T(8,128)(2,1)S(1)} collective-permute-done((bf16[64,1024]{1,0:T(8,128)(2,1)S(1)}, bf16[64,1024]{1,0:T(8,128)(2,1)S(1)}, u32[]{:S(2)}, u32[]{:S(2)}) %collective-permute-start.19) | collective-permute-done | bytes 131104 | tf_op jit(solution)/shard_map/ppermute | solution.py:412
  109.3 1.8 %collective-permute-start.21 = (bf16[64,1024]{1,0:T(8,128)(2,1)S(1)}, bf16[64,1024]{1,0:T(8,128)(2,1)S(1)}, u32[]{:S(2)}, u32[]{:S(2)}) collective-permute-start(bf16[64,1024]{1,0:T(8,128)(2,1)S(1)} %collective-permute-done.18.refs_4_), channel_id=1, source_target_pairs={{4,0},{8,4},{12,8},{16,12},{20,16},{24,20},{28,24},{0,28},{5,1},{9... | collective-permute-start | bytes 393224 | tf_op jit(solution)/shard_map/ppermute | solution.py:412
  111.2 4.3 %collective-permute-done.17.refs_3_ = bf16[64,1024]{1,0:T(8,128)(2,1)S(1)} collective-permute-done((bf16[64,1024]{1,0:T(8,128)(2,1)S(1)}, bf16[64,1024]{1,0:T(8,128)(2,1)S(1)}, u32[]{:S(2)}, u32[]{:S(2)}) %collective-permute-start.17) | collective-permute-done | bytes 131104 | tf_op jit(solution)/shard_map/ppermute | solution.py:412
  115.5 3.6 %collective-permute-done.21.refs_7_ = bf16[64,1024]{1,0:T(8,128)(2,1)S(1)} collective-permute-done((bf16[64,1024]{1,0:T(8,128)(2,1)S(1)}, bf16[64,1024]{1,0:T(8,128)(2,1)S(1)}, u32[]{:S(2)}, u32[]{:S(2)}) %collective-permute-start.21) | collective-permute-done | bytes 131104 | tf_op jit(solution)/shard_map/ppermute | solution.py:412
  119.1 1.9 %collective-permute-done.22.refs_8_ = bf16[64,1024]{1,0:T(8,128)(2,1)S(1)} collective-permute-done((bf16[64,1024]{1,0:T(8,128)(2,1)S(1)}, bf16[64,1024]{1,0:T(8,128)(2,1)S(1)}, u32[]{:S(2)}, u32[]{:S(2)}) %collective-permute-start.22) | collective-permute-done | bytes 131104 | tf_op jit(solution)/shard_map/ppermute | solution.py:412
  121.0 1.9 %shard_map.86 = (bf16[2,64,1024]{2,1,0:T(8,128)(2,1)S(1)}, bf16[2,64,1024]{2,1,0:T(8,128)(2,1)S(1)}, bf16[2,64,1024]{2,1,0:T(8,128)(2,1)S(1)}, bf16[2,64,1024]{2,1,0:T(8,128)(2,1)S(1)}) custom-call(s32[8]{0:T(128)S(1)} %stack.53.refs_0_, bf16[64,1024]{1,0:T(8,128)(2,1)S(1)} %shard_map.85.refs_1_, bf16[64,1024]{1,0:T(8,128)(2,1)S(1)} %collective-permute-done.16.refs_2_, ...), custom_call_target="tpu_custom_call" | custom-call | flops 1073741824 | bytes 4000000 | tf_op jit(solution)/shard_map/pallas_call | solution.py:391
  122.8 2.0 %collective-permute-start.25 = (bf16[2,64,1024]{2,1,0:T(8,128)(2,1)S(1)}, bf16[2,64,1024]{2,1,0:T(8,128)(2,1)S(1)}, u32[]{:S(2)}, u32[]{:S(2)}) collective-permute-start(bf16[2,64,1024]{2,1,0:T(8,128)(2,1)S(1)} %get-tuple-element.88), channel_id=1, source_target_pairs={{0,32},{32,64},{64,96},{96,0},{1,33},{33,65},{65,97},{97,1},{2,34}... | collective-permute-start | bytes 786440 | tf_op jit(solution)/shard_map/ppermute | solution.py:484
  124.8 2.8 %collective-permute-start.26 = (bf16[2,64,1024]{2,1,0:T(8,128)(2,1)S(1)}, bf16[2,64,1024]{2,1,0:T(8,128)(2,1)S(1)}, u32[]{:S(2)}, u32[]{:S(2)}) collective-permute-start(bf16[2,64,1024]{2,1,0:T(8,128)(2,1)S(1)} %get-tuple-element.89), channel_id=1, source_target_pairs={{0,64},{32,96},{64,0},{96,32},{1,65},{33,97},{65,1},{97,33},{2,66}... | collective-permute-start | bytes 786440 | tf_op jit(solution)/shard_map/ppermute | solution.py:484
  127.6 1.7 %collective-permute-start.27 = (bf16[2,64,1024]{2,1,0:T(8,128)(2,1)S(1)}, bf16[2,64,1024]{2,1,0:T(8,128)(2,1)S(1)}, u32[]{:S(2)}, u32[]{:S(2)}) collective-permute-start(bf16[2,64,1024]{2,1,0:T(8,128)(2,1)S(1)} %get-tuple-element.90), channel_id=1, source_target_pairs={{0,96},{32,0},{64,32},{96,64},{1,97},{33,1},{65,33},{97,65},{2,98}... | collective-permute-start | bytes 786440 | tf_op jit(solution)/shard_map/ppermute | solution.py:484
  129.4 3.3 %collective-permute-done.25 = bf16[2,64,1024]{2,1,0:T(8,128)(2,1)S(1)} collective-permute-done((bf16[2,64,1024]{2,1,0:T(8,128)(2,1)S(1)}, bf16[2,64,1024]{2,1,0:T(8,128)(2,1)S(1)}, u32[]{:S(2)}, u32[]{:S(2)}) %collective-permute-start.25) | collective-permute-done | bytes 262176 | tf_op jit(solution)/shard_map/ppermute | solution.py:484
  132.7 6.5 %collective-permute-done.26 = bf16[2,64,1024]{2,1,0:T(8,128)(2,1)S(1)} collective-permute-done((bf16[2,64,1024]{2,1,0:T(8,128)(2,1)S(1)}, bf16[2,64,1024]{2,1,0:T(8,128)(2,1)S(1)}, u32[]{:S(2)}, u32[]{:S(2)}) %collective-permute-start.26) | collective-permute-done | bytes 262176 | tf_op jit(solution)/shard_map/ppermute | solution.py:484
  139.2 0.2 fusion.3
  139.4 1.0 collective-permute-start.28
  140.4 4.0 %collective-permute-start.29 = (bf16[64,512]{1,0:T(8,128)(2,1)S(1)}, bf16[64,512]{1,0:T(8,128)(2,1)S(1)}, u32[]{:S(2)}, u32[]{:S(2)}) collective-permute-start(bf16[64,512]{1,0:T(8,128)(2,1)S(1)} %get-tuple-element.97), channel_id=1, source_target_pairs={{0,2},{2,0},{128,130},{130,128},{1,3},{3,1},{129,131},{131,129},{4... | collective-permute-start | bytes 196616 | tf_op jit(solution)/shard_map/ppermute | solution.py:493
  144.3 0.2 collective-permute-start.30
  144.5 2.1 %collective-permute-done.29 = bf16[64,512]{1,0:T(8,128)(2,1)S(1)} collective-permute-done((bf16[64,512]{1,0:T(8,128)(2,1)S(1)}, bf16[64,512]{1,0:T(8,128)(2,1)S(1)}, u32[]{:S(2)}, u32[]{:S(2)}) %collective-permute-start.29) | collective-permute-done | bytes 65568 | tf_op jit(solution)/shard_map/ppermute | solution.py:493
  146.6 2.8 %collective-permute-done.30 = bf16[64,512]{1,0:T(8,128)(2,1)S(1)} collective-permute-done((bf16[64,512]{1,0:T(8,128)(2,1)S(1)}, bf16[64,512]{1,0:T(8,128)(2,1)S(1)}, u32[]{:S(2)}, u32[]{:S(2)}) %collective-permute-start.30) | collective-permute-done | bytes 65568 | tf_op jit(solution)/shard_map/ppermute | solution.py:493
  149.4 2.7 %collective-permute-start.31 = (bf16[2,64,256]{2,1,0:T(8,128)(2,1)S(1)}, bf16[2,64,256]{2,1,0:T(8,128)(2,1)S(1)}, u32[]{:S(2)}, u32[]{:S(2)}) collective-permute-start(bf16[2,64,256]{2,1,0:T(8,128)(2,1)S(1)} %pad_maximum_fusion.1), channel_id=1, source_target_pairs={{0,1},{1,0},{2,3},{3,2},{4,5},{5,4},{6,7},{7,6},{8,9},{9,8},{10,11... | collective-permute-start | bytes 196616 | tf_op jit(solution)/shard_map/ppermute | solution.py:403
  152.1 0.9 collective-permute-done.31
  153.1 0.7 copy.9
  (39 shorter events, 0.6 us)
Async XLA Ops:
  0.0 13.6 %copy-start.2 = (bf16[64,1024]{1,0:T(8,128)(2,1)S(1)}, bf16[64,1024]{1,0:T(8,128)(2,1)}, u32[]{:S(2)}) copy-start(bf16[64,1024]{1,0:T(8,128)(2,1)} %refs_2_.3) | copy-start | bytes 393220
  0.0 35.1 %copy-start.1 = (s32[32768]{0:T(1024)S(1)}, s32[32768]{0:T(1024)}, u32[]{:S(2)}) copy-start(s32[32768]{0:T(1024)} %param.15) | copy-start | bytes 393220
  0.0 35.1 %copy-start.3 = (s32[2048]{0:T(1024)S(1)}, s32[2048]{0:T(1024)}, u32[]{:S(2)}) copy-start(s32[2048]{0:T(1024)} %param.14) | copy-start | bytes 24580
  2.2 27.8 %collective-permute-start.3 = (bf16[256,1024]{1,0:T(8,128)(2,1)}, bf16[256,1024]{1,0:T(8,128)(2,1)S(1)}, u32[]{:S(2)}, u32[]{:S(2)}) collective-permute-start(bf16[256,1024]{1,0:T(8,128)(2,1)} %shard_map.82.refs_7_), channel_id=1, source_target_pairs={{0,2},{2,0},{1,3},{3,1},{4,6},{6,4},{5,7},{7,5},{8,10},{10,8},{9,1... | collective-permute-start | bytes 1572872 | tf_op jit(solution)/shard_map/ppermute | solution.py:403
  6.1 24.0 %collective-permute-start.4 = (bf16[256,1024]{1,0:T(8,128)(2,1)}, bf16[256,1024]{1,0:T(8,128)(2,1)S(1)}, u32[]{:S(2)}, u32[]{:S(2)}) collective-permute-start(bf16[256,1024]{1,0:T(8,128)(2,1)} %shard_map.82.refs_7_), channel_id=1, source_target_pairs={{4,0},{6,2},{8,4},{10,6},{12,8},{5,9},{14,10},{7,11},{16,12},{9,13... | collective-permute-start | bytes 1572872 | tf_op jit(solution)/shard_map/ppermute | solution.py:434
  13.6 10.7 %collective-permute-start = (bf16[64,1024]{1,0:T(8,128)(2,1)S(1)}, bf16[64,1024]{1,0:T(8,128)(2,1)S(1)}, u32[]{:S(2)}, u32[]{:S(2)}) collective-permute-start(bf16[64,1024]{1,0:T(8,128)(2,1)S(1)} %copy-done.2), channel_id=1, source_target_pairs={{16,0},{20,4},{24,8},{28,12},{12,28},{17,1},{21,5},{25,9},{29,13},... | collective-permute-start | bytes 393224 | tf_op jit(solution)/shard_map/ppermute | solution.py:412
  14.9 14.0 %collective-permute-start.1 = (bf16[64,1024]{1,0:T(8,128)(2,1)S(1)}, bf16[64,1024]{1,0:T(8,128)(2,1)S(1)}, u32[]{:S(2)}, u32[]{:S(2)}) collective-permute-start(bf16[64,1024]{1,0:T(8,128)(2,1)S(1)} %copy-done.2), channel_id=1, source_target_pairs={{8,0},{12,4},{16,8},{20,12},{24,16},{28,20},{4,28},{9,1},{13,5},{1... | collective-permute-start | bytes 393224 | tf_op jit(solution)/shard_map/ppermute | solution.py:412
  16.2 13.8 %collective-permute-start.2 = (bf16[64,1024]{1,0:T(8,128)(2,1)S(1)}, bf16[64,1024]{1,0:T(8,128)(2,1)S(1)}, u32[]{:S(2)}, u32[]{:S(2)}) collective-permute-start(bf16[64,1024]{1,0:T(8,128)(2,1)S(1)} %copy-done.2), channel_id=1, source_target_pairs={{24,0},{28,4},{20,28},{25,1},{29,5},{21,29},{26,2},{30,6},{22,30},... | collective-permute-start | bytes 393224 | tf_op jit(solution)/shard_map/ppermute | solution.py:412
  24.3 5.7 %collective-permute-start.5 = (bf16[64,1024]{1,0:T(8,128)(2,1)S(1)}, bf16[64,1024]{1,0:T(8,128)(2,1)S(1)}, u32[]{:S(2)}, u32[]{:S(2)}) collective-permute-start(bf16[64,1024]{1,0:T(8,128)(2,1)S(1)} %copy-done.2), channel_id=1, source_target_pairs={{28,24},{29,25},{30,26},{31,27},{60,56},{61,57},{62,58},{63,59},{9... | collective-permute-start | bytes 393224 | tf_op jit(solution)/shard_map/ppermute | solution.py:450
  30.0 3.3 %collective-permute-start.9 = (bf16[256,1024]{1,0:T(8,128)(2,1)S(1)}, bf16[256,1024]{1,0:T(8,128)(2,1)S(1)}, u32[]{:S(2)}, u32[]{:S(2)}) collective-permute-start(bf16[256,1024]{1,0:T(8,128)(2,1)S(1)} %collective-permute-done.4.refs_11_), channel_id=1, source_target_pairs={{0,1},{1,0},{2,3},{3,2},{4,5},{5,4},{6,7},{7,6},{8,9},{9,8},{10,11... | collective-permute-start | bytes 1572872 | tf_op jit(solution)/shard_map/ppermute | solution.py:403
  31.8 3.2 %collective-permute-start.7 = (bf16[256,1024]{1,0:T(8,128)(2,1)}, bf16[256,1024]{1,0:T(8,128)(2,1)S(1)}, u32[]{:S(2)}, u32[]{:S(2)}) collective-permute-start(bf16[256,1024]{1,0:T(8,128)(2,1)} %shard_map.82.refs_7_), channel_id=1, source_target_pairs={{0,1},{1,0},{2,3},{3,2},{4,5},{5,4},{6,7},{7,6},{8,9},{9,8},{10,11... | collective-permute-start | bytes 1572872 | tf_op jit(solution)/shard_map/ppermute | solution.py:403
  31.9 3.1 %collective-permute-start.8 = (bf16[256,1024]{1,0:T(8,128)(2,1)S(1)}, bf16[256,1024]{1,0:T(8,128)(2,1)S(1)}, u32[]{:S(2)}, u32[]{:S(2)}) collective-permute-start(bf16[256,1024]{1,0:T(8,128)(2,1)S(1)} %collective-permute-done.3.refs_9_), channel_id=1, source_target_pairs={{0,1},{1,0},{2,3},{3,2},{4,5},{5,4},{6,7},{7,6},{8,9},{9,8},{10,11... | collective-permute-start | bytes 1572872 | tf_op jit(solution)/shard_map/ppermute | solution.py:403
  32.3 34.8 %collective-permute-start.6 = (bf16[256,1024]{1,0:T(8,128)(2,1)S(1)}, bf16[256,1024]{1,0:T(8,128)(2,1)S(1)}, u32[]{:S(2)}, u32[]{:S(2)}) collective-permute-start(bf16[256,1024]{1,0:T(8,128)(2,1)S(1)} %collective-permute-done.4.refs_11_), channel_id=1, source_target_pairs={{0,2},{2,0},{1,3},{3,1},{4,6},{6,4},{5,7},{7,5},{8,10},{10,8},{9,1... | collective-permute-start | bytes 1572872 | tf_op jit(solution)/shard_map/ppermute | solution.py:403
  35.1 1.0 copy-start
  36.1 33.2 %copy-start.4 = (bf16[1024,256]{1,0:T(8,128)(2,1)S(1)}, bf16[1024,256]{1,0:T(8,128)(2,1)}, u32[]{:S(2)}) copy-start(bf16[1024,256]{1,0:T(8,128)(2,1)} %refs_9_) | copy-start | bytes 1572868
  67.1 3.8 %collective-permute-start.11 = (bf16[256,1024]{1,0:T(8,128)(2,1)S(1)}, bf16[256,1024]{1,0:T(8,128)(2,1)S(1)}, u32[]{:S(2)}, u32[]{:S(2)}) collective-permute-start(bf16[256,1024]{1,0:T(8,128)(2,1)S(1)} %collective-permute-done.6.refs_7_), channel_id=1, source_target_pairs={{0,1},{1,0},{2,3},{3,2},{4,5},{5,4},{6,7},{7,6},{8,9},{9,8},{10,11... | collective-permute-start | bytes 1572872 | tf_op jit(solution)/shard_map/ppermute | solution.py:403
  69.3 23.2 %collective-permute-start.10 = (bf16[1024,256]{1,0:T(8,128)(2,1)S(1)}, bf16[1024,256]{1,0:T(8,128)(2,1)S(1)}, u32[]{:S(2)}, u32[]{:S(2)}) collective-permute-start(bf16[1024,256]{1,0:T(8,128)(2,1)S(1)} %copy-done.4), channel_id=1, source_target_pairs={{0,2},{2,0},{1,3},{3,1},{4,6},{6,4},{5,7},{7,5},{8,10},{10,8},{9,1... | collective-permute-start | bytes 1572872 | tf_op jit(solution)/shard_map/ppermute | solution.py:403
  77.3 8.0 %collective-permute-start.12 = (bf16[64,1152]{1,0:T(8,128)(2,1)S(1)}, bf16[64,1152]{1,0:T(8,128)(2,1)S(1)}, u32[]{:S(2)}, u32[]{:S(2)}) collective-permute-start(bf16[64,1152]{1,0:T(8,128)(2,1)S(1)} %get-tuple-element.82), channel_id=1, source_target_pairs={{0,16},{4,20},{8,24},{12,28},{28,12},{1,17},{5,21},{9,25},{13,29},... | collective-permute-start | bytes 442376 | tf_op jit(solution)/shard_map/ppermute | solution.py:417
  78.6 6.8 %collective-permute-start.13 = (bf16[64,1152]{1,0:T(8,128)(2,1)S(1)}, bf16[64,1152]{1,0:T(8,128)(2,1)S(1)}, u32[]{:S(2)}, u32[]{:S(2)}) collective-permute-start(bf16[64,1152]{1,0:T(8,128)(2,1)S(1)} %get-tuple-element.83), channel_id=1, source_target_pairs={{0,8},{4,12},{8,16},{12,20},{16,24},{20,28},{28,4},{1,9},{5,13},{9... | collective-permute-start | bytes 442376 | tf_op jit(solution)/shard_map/ppermute | solution.py:417
  83.3 8.5 %collective-permute-start.14 = (bf16[64,1152]{1,0:T(8,128)(2,1)S(1)}, bf16[64,1152]{1,0:T(8,128)(2,1)S(1)}, u32[]{:S(2)}, u32[]{:S(2)}) collective-permute-start(bf16[64,1152]{1,0:T(8,128)(2,1)S(1)} %get-tuple-element.84), channel_id=1, source_target_pairs={{0,24},{4,28},{28,20},{1,25},{5,29},{29,21},{2,26},{6,30},{30,22},... | collective-permute-start | bytes 442376 | tf_op jit(solution)/shard_map/ppermute | solution.py:417
  84.6 7.2 %collective-permute-start.15 = (bf16[64,1152]{1,0:T(8,128)(2,1)S(1)}, bf16[64,1152]{1,0:T(8,128)(2,1)S(1)}, u32[]{:S(2)}, u32[]{:S(2)}) collective-permute-start(bf16[64,1152]{1,0:T(8,128)(2,1)S(1)} %get-tuple-element.83), channel_id=1, source_target_pairs={{24,28},{25,29},{26,30},{27,31},{56,60},{57,61},{58,62},{59,63},{8... | collective-permute-start | bytes 442376 | tf_op jit(solution)/shard_map/ppermute | solution.py:471
  85.3 19.1 %collective-permute-start.23 = (bf16[1024,256]{1,0:T(8,128)(2,1)S(1)}, bf16[1024,256]{1,0:T(8,128)(2,1)S(1)}, u32[]{:S(2)}, u32[]{:S(2)}) collective-permute-start(bf16[1024,256]{1,0:T(8,128)(2,1)S(1)} %copy-done.4), channel_id=1, source_target_pairs={{0,1},{1,0},{2,3},{3,2},{4,5},{5,4},{6,7},{7,6},{8,9},{9,8},{10,11... | collective-permute-start | bytes 1572872 | tf_op jit(solution)/shard_map/ppermute | solution.py:403
  92.5 28.4 %collective-permute-start.24 = (bf16[1024,256]{1,0:T(8,128)(2,1)S(1)}, bf16[1024,256]{1,0:T(8,128)(2,1)S(1)}, u32[]{:S(2)}, u32[]{:S(2)}) collective-permute-start(bf16[1024,256]{1,0:T(8,128)(2,1)S(1)} %collective-permute-done.10.refs_11_), channel_id=1, source_target_pairs={{0,1},{1,0},{2,3},{3,2},{4,5},{5,4},{6,7},{7,6},{8,9},{9,8},{10,11... | collective-permute-start | bytes 1572872 | tf_op jit(solution)/shard_map/ppermute | solution.py:403
  92.6 11.8 %collective-permute-start.18 = (bf16[64,1024]{1,0:T(8,128)(2,1)S(1)}, bf16[64,1024]{1,0:T(8,128)(2,1)S(1)}, u32[]{:S(2)}, u32[]{:S(2)}) collective-permute-start(bf16[64,1024]{1,0:T(8,128)(2,1)S(1)} %shard_map.85.refs_1_), channel_id=1, source_target_pairs={{8,0},{12,4},{16,8},{20,12},{24,16},{28,20},{0,24},{4,28},{9,1},{1... | collective-permute-start | bytes 393224 | tf_op jit(solution)/shard_map/ppermute | solution.py:412
  99.8 9.5 %collective-permute-start.19 = (bf16[64,1024]{1,0:T(8,128)(2,1)S(1)}, bf16[64,1024]{1,0:T(8,128)(2,1)S(1)}, u32[]{:S(2)}, u32[]{:S(2)}) collective-permute-start(bf16[64,1024]{1,0:T(8,128)(2,1)S(1)} %shard_map.85.refs_1_), channel_id=1, source_target_pairs={{24,0},{28,4},{0,8},{4,12},{8,16},{12,20},{16,24},{20,28},{25,1},{... | collective-permute-start | bytes 393224 | tf_op jit(solution)/shard_map/ppermute | solution.py:412
  99.8 11.3 %collective-permute-start.16 = (bf16[64,1024]{1,0:T(8,128)(2,1)S(1)}, bf16[64,1024]{1,0:T(8,128)(2,1)S(1)}, u32[]{:S(2)}, u32[]{:S(2)}) collective-permute-start(bf16[64,1024]{1,0:T(8,128)(2,1)S(1)} %shard_map.85.refs_1_), channel_id=1, source_target_pairs={{4,0},{8,4},{12,8},{16,12},{20,16},{24,20},{28,24},{0,28},{5,1},{9... | collective-permute-start | bytes 393224 | tf_op jit(solution)/shard_map/ppermute | solution.py:412
  104.4 11.1 %collective-permute-start.17 = (bf16[64,1024]{1,0:T(8,128)(2,1)S(1)}, bf16[64,1024]{1,0:T(8,128)(2,1)S(1)}, u32[]{:S(2)}, u32[]{:S(2)}) collective-permute-start(bf16[64,1024]{1,0:T(8,128)(2,1)S(1)} %shard_map.85.refs_1_), channel_id=1, source_target_pairs={{28,0},{0,4},{4,8},{8,12},{12,16},{16,20},{20,24},{24,28},{29,1},{... | collective-permute-start | bytes 393224 | tf_op jit(solution)/shard_map/ppermute | solution.py:412
  104.4 11.1 %collective-permute-start.20 = (bf16[64,1024]{1,0:T(8,128)(2,1)S(1)}, bf16[64,1024]{1,0:T(8,128)(2,1)S(1)}, u32[]{:S(2)}, u32[]{:S(2)}) collective-permute-start(bf16[64,1024]{1,0:T(8,128)(2,1)S(1)} %shard_map.85.refs_1_), channel_id=1, source_target_pairs={{16,0},{20,4},{24,8},{28,12},{0,16},{4,20},{8,24},{12,28},{17,1},{... | collective-permute-start | bytes 393224 | tf_op jit(solution)/shard_map/ppermute | solution.py:412
  109.3 9.8 %collective-permute-start.21 = (bf16[64,1024]{1,0:T(8,128)(2,1)S(1)}, bf16[64,1024]{1,0:T(8,128)(2,1)S(1)}, u32[]{:S(2)}, u32[]{:S(2)}) collective-permute-start(bf16[64,1024]{1,0:T(8,128)(2,1)S(1)} %collective-permute-done.18.refs_4_), channel_id=1, source_target_pairs={{4,0},{8,4},{12,8},{16,12},{20,16},{24,20},{28,24},{0,28},{5,1},{9... | collective-permute-start | bytes 393224 | tf_op jit(solution)/shard_map/ppermute | solution.py:412
  111.1 9.9 %collective-permute-start.22 = (bf16[64,1024]{1,0:T(8,128)(2,1)S(1)}, bf16[64,1024]{1,0:T(8,128)(2,1)S(1)}, u32[]{:S(2)}, u32[]{:S(2)}) collective-permute-start(bf16[64,1024]{1,0:T(8,128)(2,1)S(1)} %collective-permute-done.19.refs_5_), channel_id=1, source_target_pairs={{28,0},{0,4},{4,8},{8,12},{12,16},{16,20},{20,24},{24,28},{29,1},{... | collective-permute-start | bytes 393224 | tf_op jit(solution)/shard_map/ppermute | solution.py:412
  122.8 9.9 %collective-permute-start.25 = (bf16[2,64,1024]{2,1,0:T(8,128)(2,1)S(1)}, bf16[2,64,1024]{2,1,0:T(8,128)(2,1)S(1)}, u32[]{:S(2)}, u32[]{:S(2)}) collective-permute-start(bf16[2,64,1024]{2,1,0:T(8,128)(2,1)S(1)} %get-tuple-element.88), channel_id=1, source_target_pairs={{0,32},{32,64},{64,96},{96,0},{1,33},{33,65},{65,97},{97,1},{2,34}... | collective-permute-start | bytes 786440 | tf_op jit(solution)/shard_map/ppermute | solution.py:484
  124.8 14.4 %collective-permute-start.26 = (bf16[2,64,1024]{2,1,0:T(8,128)(2,1)S(1)}, bf16[2,64,1024]{2,1,0:T(8,128)(2,1)S(1)}, u32[]{:S(2)}, u32[]{:S(2)}) collective-permute-start(bf16[2,64,1024]{2,1,0:T(8,128)(2,1)S(1)} %get-tuple-element.89), channel_id=1, source_target_pairs={{0,64},{32,96},{64,0},{96,32},{1,65},{33,97},{65,1},{97,33},{2,66}... | collective-permute-start | bytes 786440 | tf_op jit(solution)/shard_map/ppermute | solution.py:484
  127.6 11.5 %collective-permute-start.27 = (bf16[2,64,1024]{2,1,0:T(8,128)(2,1)S(1)}, bf16[2,64,1024]{2,1,0:T(8,128)(2,1)S(1)}, u32[]{:S(2)}, u32[]{:S(2)}) collective-permute-start(bf16[2,64,1024]{2,1,0:T(8,128)(2,1)S(1)} %get-tuple-element.90), channel_id=1, source_target_pairs={{0,96},{32,0},{64,32},{96,64},{1,97},{33,1},{65,33},{97,65},{2,98}... | collective-permute-start | bytes 786440 | tf_op jit(solution)/shard_map/ppermute | solution.py:484
  139.4 5.2 %collective-permute-start.28 = (bf16[64,512]{1,0:T(8,128)(2,1)S(1)}, bf16[64,512]{1,0:T(8,128)(2,1)S(1)}, u32[]{:S(2)}, u32[]{:S(2)}) collective-permute-start(bf16[64,512]{1,0:T(8,128)(2,1)S(1)} %get-tuple-element.95), channel_id=1, source_target_pairs={{0,128},{2,130},{128,0},{130,2},{1,129},{3,131},{129,1},{131,3},{4... | collective-permute-start | bytes 196616 | tf_op jit(solution)/shard_map/ppermute | solution.py:493
  140.4 6.2 %collective-permute-start.29 = (bf16[64,512]{1,0:T(8,128)(2,1)S(1)}, bf16[64,512]{1,0:T(8,128)(2,1)S(1)}, u32[]{:S(2)}, u32[]{:S(2)}) collective-permute-start(bf16[64,512]{1,0:T(8,128)(2,1)S(1)} %get-tuple-element.97), channel_id=1, source_target_pairs={{0,2},{2,0},{128,130},{130,128},{1,3},{3,1},{129,131},{131,129},{4... | collective-permute-start | bytes 196616 | tf_op jit(solution)/shard_map/ppermute | solution.py:493
  144.3 5.0 %collective-permute-start.30 = (bf16[64,512]{1,0:T(8,128)(2,1)S(1)}, bf16[64,512]{1,0:T(8,128)(2,1)S(1)}, u32[]{:S(2)}, u32[]{:S(2)}) collective-permute-start(bf16[64,512]{1,0:T(8,128)(2,1)S(1)} %get-tuple-element.96), channel_id=1, source_target_pairs={{0,130},{2,128},{128,2},{130,0},{1,131},{3,129},{129,3},{131,1},{4... | collective-permute-start | bytes 196616 | tf_op jit(solution)/shard_map/ppermute | solution.py:493
  149.4 3.6 %collective-permute-start.31 = (bf16[2,64,256]{2,1,0:T(8,128)(2,1)S(1)}, bf16[2,64,256]{2,1,0:T(8,128)(2,1)S(1)}, u32[]{:S(2)}, u32[]{:S(2)}) collective-permute-start(bf16[2,64,256]{2,1,0:T(8,128)(2,1)S(1)} %pad_maximum_fusion.1), channel_id=1, source_target_pairs={{0,1},{1,0},{2,3},{3,2},{4,5},{5,4},{6,7},{7,6},{8,9},{9,8},{10,11... | collective-permute-start | bytes 196616 | tf_op jit(solution)/shard_map/ppermute | solution.py:403

commit v2 on v0

--- a/solution.py
+++ b/solution.py
@@ -467,9 +467,11 @@
     w_y, attended = lax.optimization_barrier((w_y, attended))
     ws = [out_weight, swap(out_weight, "core"), w_y, swap(w_y, "core")]
 
-    up, down = fetch(attended, 1, False), fetch(attended, NZ - 1, False)
     up2, down2, far = [fetch(attended, k, False) for k in SHIFTS[1:]]
-    blocks = [attended, up, down, up2, down2, far, fetch(up2, 1, False), fetch(down2, NZ - 1, False)]
+    above = fetch(jnp.concatenate([attended, up2], axis=0), 1, False)
+    below = fetch(jnp.concatenate([attended, down2], axis=0), NZ - 1, False)
+    blocks = [attended, above[:tokens], below[:tokens], up2, down2, far]
+    blocks += [above[tokens:], below[tokens:]]
     planes = [(z + k) % NZ for k in (0, 1, 7, 2, 6, 4, 3, 5)]
     slots = [2 * ((p % 4 - x) % 4) + ((p // 4) ^ yl) for p in planes]
     outs = project(jnp.stack(slots).astype(jnp.int32), blocks, ws, 4)

time: 155 us -> 150 us (0.968)
  starting transfers between devices: 96.6 us -> 61 us
  Pallas kernels: 19 us -> 38.6 us
  waiting for transfers between devices: 38.9 us -> 49.9 us
    ppermute x10 -> x8, starting transfers between devices: 43.5 us -> 16.2 us  [fetch(): return lax.ppermute(array, 'z', pairs)]
    pallas_call x2, Pallas kernels: 14.2 us -> 33.8 us  [flash(): pl.pallas_call(functools.partial(flash_kernel, nq, nk, first, last, group...]
    ppermute x3, starting transfers between devices: 13.9 us -> 6.76 us  [give(): return lax.ppermute(array, 'z', pairs)]
    ppermute x10 -> x8, waiting for transfers between devices: 20.9 us -> 26.5 us  [fetch(): return lax.ppermute(array, 'z', pairs)]
    ppermute x3, waiting for transfers between devices: 1.43 us -> 5.76 us  [give(): return lax.ppermute(array, 'z', pairs)]
    ppermute x3, starting transfers between devices: 6.94 us -> 4.32 us  [along_x(): return lax.ppermute(array, 'x', [(n, (n + k) % 4) for n in range(4)])]
  transfers between devices with their start and end apart: 32 -> 30, of which waited for: 18 -> 20; matrix products, arithmetic and copies ran while one was open for 0% -> 0% of each run, Pallas kernels for 10% -> 23%
where the time goes in v2:
time: 150 us; the launch traced here: 152 us
  starting transfers between devices  61 us (41%)
  waiting for transfers between devices  49.9 us (33%)
  Pallas kernels  38.6 us (26%)
  local copies, waits for them, and re-layouts  1.86 us (1%)
    pallas_call x2, Pallas kernels, flash(): pl.pallas_call(functools.partial(flash_kernel, nq, nk, first, last, group...  33.8 us
    ppermute x8, waiting for transfers between devices, fetch(): return lax.ppermute(array, 'z', pairs)  26.5 us
    ppermute x10, starting transfers between devices, swap(): return lax.ppermute(array, axis, [(0, 1), (1, 0)])  21 us
    ppermute x8, starting transfers between devices, fetch(): return lax.ppermute(array, 'z', pairs)  16.2 us
    ppermute x3, waiting for transfers between devices, along_x(): return lax.ppermute(array, 'x', [(n, (n + k) % 4) for n in range(4)])  10.4 us
    ppermute x1, starting transfers between devices, beside(): return lax.ppermute(array, ('z', 'yh', 'core'), pairs)  7.5 us
    ppermute x3, starting transfers between devices, give(): return lax.ppermute(array, 'z', pairs)  6.76 us
    ppermute x3, waiting for transfers between devices, give(): return lax.ppermute(array, 'z', pairs)  5.76 us
  transfers between devices with their start and end apart: 30, of which 20 were waited for; matrix products, arithmetic and copies ran while one was open for 0% of the time, Pallas kernels for 23%

profile of v2, /device:TPU:1, one launch (start us, length us, event | category | flops | bytes accessed | tf_op | source)
XLA Modules:
  0.0 152.0 jit_solution(1477967922434246304)
XLA Ops:
  0.0 2.2 %shard_map.82.refs_7_ = bf16[256,1024]{1,0:T(8,128)(2,1)} custom-call(bf16[1024,128]{1,0:T(8,128)(2,1)} %lk_in.1, bf16[1024,128]{1,0:T(8,128)(2,1)} %lv_in.1, bf16[1,128,128]{2,1,0:T(8,128)(2,1)} %bk_in.1, bf16[1,128,128]{2,1,0:T(8,128)(2,1)} %bv_in.1), custom_call_target="tpu_custom_call" | custom-call | flops 67108864 | bytes 1048576 | tf_op jit(solution)/shard_map/pallas_call | solution.py:54
  2.3 3.8 %collective-permute-start = (bf16[256,1024]{1,0:T(8,128)(2,1)}, bf16[256,1024]{1,0:T(8,128)(2,1)S(1)}, u32[]{:S(2)}, u32[]{:S(2)}) collective-permute-start(bf16[256,1024]{1,0:T(8,128)(2,1)} %shard_map.82.refs_7_), channel_id=1, source_target_pairs={{0,2},{2,0},{1,3},{3,1},{4,6},{6,4},{5,7},{7,5},{8,10},{10,8},{9,1... | collective-permute-start | bytes 1572872 | tf_op jit(solution)/shard_map/ppermute | solution.py:401
  6.1 7.5 %collective-permute-start.1 = (bf16[256,1024]{1,0:T(8,128)(2,1)}, bf16[256,1024]{1,0:T(8,128)(2,1)S(1)}, u32[]{:S(2)}, u32[]{:S(2)}) collective-permute-start(bf16[256,1024]{1,0:T(8,128)(2,1)} %shard_map.82.refs_7_), channel_id=1, source_target_pairs={{4,0},{6,2},{8,4},{10,6},{12,8},{5,9},{14,10},{7,11},{16,12},{9,13... | collective-permute-start | bytes 1572872 | tf_op jit(solution)/shard_map/ppermute | solution.py:432
  13.6 0.7 collective-permute-start.2
  14.3 1.3 collective-permute-start.3
  15.6 1.3 collective-permute-start.4
  16.9 1.3 collective-permute-start.5
  18.2 3.6 %collective-permute-done.3.refs_3_ = bf16[64,1024]{1,0:T(8,128)(2,1)S(1)} collective-permute-done((bf16[64,1024]{1,0:T(8,128)(2,1)S(1)}, bf16[64,1024]{1,0:T(8,128)(2,1)S(1)}, u32[]{:S(2)}, u32[]{:S(2)}) %collective-permute-start.3) | collective-permute-done | bytes 131104 | tf_op jit(solution)/shard_map/ppermute | solution.py:410
  21.8 3.6 %collective-permute-done.4.refs_4_ = bf16[64,1024]{1,0:T(8,128)(2,1)S(1)} collective-permute-done((bf16[64,1024]{1,0:T(8,128)(2,1)S(1)}, bf16[64,1024]{1,0:T(8,128)(2,1)S(1)}, u32[]{:S(2)}, u32[]{:S(2)}) %collective-permute-start.4) | collective-permute-done | bytes 131104 | tf_op jit(solution)/shard_map/ppermute | solution.py:410
  25.3 1.4 collective-permute-done.5.refs_5_
  26.9 5.5 %collective-permute-start.9 = (bf16[256,1024]{1,0:T(8,128)(2,1)S(1)}, bf16[256,1024]{1,0:T(8,128)(2,1)S(1)}, u32[]{:S(2)}, u32[]{:S(2)}) collective-permute-start(bf16[256,1024]{1,0:T(8,128)(2,1)S(1)} %collective-permute-done.1.refs_11_), channel_id=1, source_target_pairs={{0,1},{1,0},{2,3},{3,2},{4,5},{5,4},{6,7},{7,6},{8,9},{9,8},{10,11... | collective-permute-start | bytes 1572872 | tf_op jit(solution)/shard_map/ppermute | solution.py:401
  32.5 0.4 collective-permute-start.8
  33.0 1.0 collective-permute-done.9.refs_12_
  34.0 1.7 %collective-permute-done.7.refs_8_ = bf16[256,1024]{1,0:T(8,128)(2,1)S(1)} collective-permute-done((bf16[256,1024]{1,0:T(8,128)(2,1)}, bf16[256,1024]{1,0:T(8,128)(2,1)S(1)}, u32[]{:S(2)}, u32[]{:S(2)}) %collective-permute-start.7) | collective-permute-done | bytes 524320 | tf_op jit(solution)/shard_map/ppermute | solution.py:401
  35.7 1.0 copy-done
  36.7 28.6 %shard_map.83 = (f32[8,512]{1,0:T(8,128)S(1)}, f32[8,512]{1,0:T(8,128)S(1)}, f32[128,512]{1,0:T(8,128)S(1)}, f32[8,512]{1,0:T(8,128)S(1)}, f32[8,512]{1,0:T(8,12...) custom-call(s32[256,128]{1,0:T(8,128)S(1)} %bitcast.35, ...), custom_call_target="tpu_custom_call" | custom-call | flops 1000000 | bytes 100000 | tf_op jit(solution)/shard_map/pallas_call | solution.py:318
  65.4 7.3 %collective-permute-start.11 = (bf16[256,1024]{1,0:T(8,128)(2,1)S(1)}, bf16[256,1024]{1,0:T(8,128)(2,1)S(1)}, u32[]{:S(2)}, u32[]{:S(2)}) collective-permute-start(bf16[256,1024]{1,0:T(8,128)(2,1)S(1)} %collective-permute-done.6.refs_7_), channel_id=1, source_target_pairs={{0,1},{1,0},{2,3},{3,2},{4,5},{5,4},{6,7},{7,6},{8,9},{9,8},{10,11... | collective-permute-start | bytes 1572872 | tf_op jit(solution)/shard_map/ppermute | solution.py:401
  72.7 1.5 %collective-permute-done.11.refs_8_ = bf16[256,1024]{1,0:T(8,128)(2,1)S(1)} collective-permute-done((bf16[256,1024]{1,0:T(8,128)(2,1)S(1)}, bf16[256,1024]{1,0:T(8,128)(2,1)S(1)}, u32[]{:S(2)}, u32[]{:S(2)}) %collective-permute-start.11) | collective-permute-done | bytes 524320 | tf_op jit(solution)/shard_map/ppermute | solution.py:401
  74.2 5.2 %shard_map.84 = (bf16[64,1152]{1,0:T(8,128)(2,1)S(1)}, bf16[64,1152]{1,0:T(8,128)(2,1)S(1)}, bf16[64,1152]{1,0:T(8,128)(2,1)S(1)}, bf16[64,1152]{1,0:T(8,128)(2,1)S(1)}) custom-call(s32[256,128]{1,0:T(8,128)S(1)} %bitcast.36, s32[16,128]{1,0:T(8,128)S(1)} %bitcast.38, bf16[64,1024]{1,0:T(8,128)(2,1)S(1)} %copy-done.2, ...), custom_call_target="tpu_custom_call" | custom-call | flops 1000000 | bytes 100000 | tf_op jit(solution)/shard_map/pallas_call | solution.py:318
  79.4 1.3 collective-permute-start.12
  80.7 4.2 %collective-permute-start.13 = (bf16[64,1152]{1,0:T(8,128)(2,1)S(1)}, bf16[64,1152]{1,0:T(8,128)(2,1)S(1)}, u32[]{:S(2)}, u32[]{:S(2)}) collective-permute-start(bf16[64,1152]{1,0:T(8,128)(2,1)S(1)} %get-tuple-element.89), channel_id=1, source_target_pairs={{0,8},{4,12},{8,16},{12,20},{16,24},{20,28},{28,4},{1,9},{5,13},{9... | collective-permute-start | bytes 442376 | tf_op jit(solution)/shard_map/ppermute | solution.py:415
  84.9 1.3 collective-permute-start.14
  86.2 0.7 collective-permute-start.15
  86.9 4.2 %collective-permute-done.13.refs_2_ = bf16[64,1152]{1,0:T(8,128)(2,1)S(1)} collective-permute-done((bf16[64,1152]{1,0:T(8,128)(2,1)S(1)}, bf16[64,1152]{1,0:T(8,128)(2,1)S(1)}, u32[]{:S(2)}, u32[]{:S(2)}) %collective-permute-start.13) | collective-permute-done | bytes 147488 | tf_op jit(solution)/shard_map/ppermute | solution.py:415
  91.1 1.5 %collective-permute-done.14.refs_3_ = bf16[64,1152]{1,0:T(8,128)(2,1)S(1)} collective-permute-done((bf16[64,1152]{1,0:T(8,128)(2,1)S(1)}, bf16[64,1152]{1,0:T(8,128)(2,1)S(1)}, u32[]{:S(2)}, u32[]{:S(2)}) %collective-permute-start.14) | collective-permute-done | bytes 147488 | tf_op jit(solution)/shard_map/ppermute | solution.py:415
  92.6 0.7 shard_map.85.refs_1_
  93.4 6.1 %collective-permute-start.16 = (bf16[64,1024]{1,0:T(8,128)(2,1)S(1)}, bf16[64,1024]{1,0:T(8,128)(2,1)S(1)}, u32[]{:S(2)}, u32[]{:S(2)}) collective-permute-start(bf16[64,1024]{1,0:T(8,128)(2,1)S(1)} %shard_map.85.refs_1_), channel_id=1, source_target_pairs={{8,0},{12,4},{16,8},{20,12},{24,16},{28,20},{0,24},{4,28},{9,1},{1... | collective-permute-start | bytes 393224 | tf_op jit(solution)/shard_map/ppermute | solution.py:410
  99.5 2.1 %collective-permute-done.16.refs_4_ = bf16[64,1024]{1,0:T(8,128)(2,1)S(1)} collective-permute-done((bf16[64,1024]{1,0:T(8,128)(2,1)S(1)}, bf16[64,1024]{1,0:T(8,128)(2,1)S(1)}, u32[]{:S(2)}, u32[]{:S(2)}) %collective-permute-start.16) | collective-permute-done | bytes 131104 | tf_op jit(solution)/shard_map/ppermute | solution.py:410
  101.6 4.6 %collective-permute-done.18.refs_5_ = bf16[64,1024]{1,0:T(8,128)(2,1)S(1)} collective-permute-done((bf16[64,1024]{1,0:T(8,128)(2,1)S(1)}, bf16[64,1024]{1,0:T(8,128)(2,1)S(1)}, u32[]{:S(2)}, u32[]{:S(2)}) %collective-permute-start.18) | collective-permute-done | bytes 131104 | tf_op jit(solution)/shard_map/ppermute | solution.py:410
  106.3 4.3 %collective-permute-start.19 = (bf16[128,1024]{1,0:T(8,128)(2,1)S(1)}, bf16[128,1024]{1,0:T(8,128)(2,1)S(1)}, u32[]{:S(2)}, u32[]{:S(2)}) collective-permute-start(bf16[128,1024]{1,0:T(8,128)(2,1)S(1)} %get-tuple-element.110), channel_id=1, source_target_pairs={{28,0},{0,4},{4,8},{8,12},{12,16},{16,20},{20,24},{24,28},{29,1},{... | collective-permute-start | bytes 786440 | tf_op jit(solution)/shard_map/ppermute | solution.py:410
  110.6 1.0 collective-permute-start.21
  111.6 1.5 collective-permute-start.17
  113.1 0.4 collective-permute-start.20
  113.5 2.0 %collective-permute-done.19 = bf16[128,1024]{1,0:T(8,128)(2,1)S(1)} collective-permute-done((bf16[128,1024]{1,0:T(8,128)(2,1)S(1)}, bf16[128,1024]{1,0:T(8,128)(2,1)S(1)}, u32[]{:S(2)}, u32[]{:S(2)}) %collective-permute-start.19) | collective-permute-done | bytes 262176 | tf_op jit(solution)/shard_map/ppermute | solution.py:410
  115.6 5.8 %collective-permute-done.17 = bf16[128,1024]{1,0:T(8,128)(2,1)S(1)} collective-permute-done((bf16[128,1024]{1,0:T(8,128)(2,1)S(1)}, bf16[128,1024]{1,0:T(8,128)(2,1)S(1)}, u32[]{:S(2)}, u32[]{:S(2)}) %collective-permute-start.17) | collective-permute-done | bytes 262176 | tf_op jit(solution)/shard_map/ppermute | solution.py:410
  121.4 3.5 %collective-permute-done.20.refs_6_ = bf16[64,1024]{1,0:T(8,128)(2,1)S(1)} collective-permute-done((bf16[64,1024]{1,0:T(8,128)(2,1)S(1)}, bf16[64,1024]{1,0:T(8,128)(2,1)S(1)}, u32[]{:S(2)}, u32[]{:S(2)}) %collective-permute-start.20) | collective-permute-done | bytes 131104 | tf_op jit(solution)/shard_map/ppermute | solution.py:410
  124.9 1.9 %shard_map.86 = (bf16[2,64,1024]{2,1,0:T(8,128)(2,1)S(1)}, bf16[2,64,1024]{2,1,0:T(8,128)(2,1)S(1)}, bf16[2,64,1024]{2,1,0:T(8,128)(2,1)S(1)}, bf16[2,64,1024]{2,1,0:T(8,128)(2,1)S(1)}) custom-call(s32[8]{0:T(128)S(1)} %stack.53.refs_0_, bf16[64,1024]{1,0:T(8,128)(2,1)S(1)} %shard_map.85.refs_1_, bf16[64,1024]{1,0:T(8,128)(2,1)S(1)} %get-tuple-element.107.refs_2_, ...), custom_call_target="tpu_custom_call" | custom-call | flops 1073741824 | bytes 4000000 | tf_op jit(solution)/shard_map/pallas_call | solution.py:389
  126.8 2.3 %collective-permute-start.24 = (bf16[2,64,1024]{2,1,0:T(8,128)(2,1)S(1)}, bf16[2,64,1024]{2,1,0:T(8,128)(2,1)S(1)}, u32[]{:S(2)}, u32[]{:S(2)}) collective-permute-start(bf16[2,64,1024]{2,1,0:T(8,128)(2,1)S(1)} %get-tuple-element.95), channel_id=1, source_target_pairs={{0,64},{32,96},{64,0},{96,32},{1,65},{33,97},{65,1},{97,33},{2,66}... | collective-permute-start | bytes 786440 | tf_op jit(solution)/shard_map/ppermute | solution.py:480
  129.1 2.0 %collective-permute-start.25 = (bf16[2,64,1024]{2,1,0:T(8,128)(2,1)S(1)}, bf16[2,64,1024]{2,1,0:T(8,128)(2,1)S(1)}, u32[]{:S(2)}, u32[]{:S(2)}) collective-permute-start(bf16[2,64,1024]{2,1,0:T(8,128)(2,1)S(1)} %get-tuple-element.96), channel_id=1, source_target_pairs={{0,96},{32,0},{64,32},{96,64},{1,97},{33,1},{65,33},{97,65},{2,98}... | collective-permute-start | bytes 786440 | tf_op jit(solution)/shard_map/ppermute | solution.py:480
  131.1 5.5 %collective-permute-done.23 = bf16[2,64,1024]{2,1,0:T(8,128)(2,1)S(1)} collective-permute-done((bf16[2,64,1024]{2,1,0:T(8,128)(2,1)S(1)}, bf16[2,64,1024]{2,1,0:T(8,128)(2,1)S(1)}, u32[]{:S(2)}, u32[]{:S(2)}) %collective-permute-start.23) | collective-permute-done | bytes 262176 | tf_op jit(solution)/shard_map/ppermute | solution.py:480
  136.6 3.3 %collective-permute-done.24 = bf16[2,64,1024]{2,1,0:T(8,128)(2,1)S(1)} collective-permute-done((bf16[2,64,1024]{2,1,0:T(8,128)(2,1)S(1)}, bf16[2,64,1024]{2,1,0:T(8,128)(2,1)S(1)}, u32[]{:S(2)}, u32[]{:S(2)}) %collective-permute-start.24) | collective-permute-done | bytes 262176 | tf_op jit(solution)/shard_map/ppermute | solution.py:480
  139.9 1.6 %collective-permute-done.25 = bf16[2,64,1024]{2,1,0:T(8,128)(2,1)S(1)} collective-permute-done((bf16[2,64,1024]{2,1,0:T(8,128)(2,1)S(1)}, bf16[2,64,1024]{2,1,0:T(8,128)(2,1)S(1)}, u32[]{:S(2)}, u32[]{:S(2)}) %collective-permute-start.25) | collective-permute-done | bytes 262176 | tf_op jit(solution)/shard_map/ppermute | solution.py:480
  141.8 3.7 %collective-permute-start.28 = (bf16[64,512]{1,0:T(8,128)(2,1)S(1)}, bf16[64,512]{1,0:T(8,128)(2,1)S(1)}, u32[]{:S(2)}, u32[]{:S(2)}) collective-permute-start(bf16[64,512]{1,0:T(8,128)(2,1)S(1)} %get-tuple-element.102), channel_id=1, source_target_pairs={{0,130},{2,128},{128,2},{130,0},{1,131},{3,129},{129,3},{131,1},{4... | collective-permute-start | bytes 196616 | tf_op jit(solution)/shard_map/ppermute | solution.py:489
  145.6 0.9 collective-permute-done.27
  146.4 1.1 collective-permute-done.28
  147.5 2.8 %collective-permute-start.29 = (bf16[2,64,256]{2,1,0:T(8,128)(2,1)S(1)}, bf16[2,64,256]{2,1,0:T(8,128)(2,1)S(1)}, u32[]{:S(2)}, u32[]{:S(2)}) collective-permute-start(bf16[2,64,256]{2,1,0:T(8,128)(2,1)S(1)} %pad_maximum_fusion.3), channel_id=1, source_target_pairs={{0,1},{1,0},{2,3},{3,2},{4,5},{5,4},{6,7},{7,6},{8,9},{9,8},{10,11... | collective-permute-start | bytes 196616 | tf_op jit(solution)/shard_map/ppermute | solution.py:401
  150.4 0.9 collective-permute-done.29
  151.3 0.7 copy.9
  (38 shorter events, 1.1 us)
Async XLA Ops:
  0.0 13.6 %copy-start.2 = (bf16[64,1024]{1,0:T(8,128)(2,1)S(1)}, bf16[64,1024]{1,0:T(8,128)(2,1)}, u32[]{:S(2)}) copy-start(bf16[64,1024]{1,0:T(8,128)(2,1)} %refs_2_.1) | copy-start | bytes 393220
  0.0 35.7 %copy-start.1 = (s32[32768]{0:T(1024)S(1)}, s32[32768]{0:T(1024)}, u32[]{:S(2)}) copy-start(s32[32768]{0:T(1024)} %param.15) | copy-start | bytes 393220
  0.0 35.7 %copy-start.3 = (s32[2048]{0:T(1024)S(1)}, s32[2048]{0:T(1024)}, u32[]{:S(2)}) copy-start(s32[2048]{0:T(1024)} %param.14) | copy-start | bytes 24580
  2.3 24.5 %collective-permute-start = (bf16[256,1024]{1,0:T(8,128)(2,1)}, bf16[256,1024]{1,0:T(8,128)(2,1)S(1)}, u32[]{:S(2)}, u32[]{:S(2)}) collective-permute-start(bf16[256,1024]{1,0:T(8,128)(2,1)} %shard_map.82.refs_7_), channel_id=1, source_target_pairs={{0,2},{2,0},{1,3},{3,1},{4,6},{6,4},{5,7},{7,5},{8,10},{10,8},{9,1... | collective-permute-start | bytes 1572872 | tf_op jit(solution)/shard_map/ppermute | solution.py:401
  6.1 20.9 %collective-permute-start.1 = (bf16[256,1024]{1,0:T(8,128)(2,1)}, bf16[256,1024]{1,0:T(8,128)(2,1)S(1)}, u32[]{:S(2)}, u32[]{:S(2)}) collective-permute-start(bf16[256,1024]{1,0:T(8,128)(2,1)} %shard_map.82.refs_7_), channel_id=1, source_target_pairs={{4,0},{6,2},{8,4},{10,6},{12,8},{5,9},{14,10},{7,11},{16,12},{9,13... | collective-permute-start | bytes 1572872 | tf_op jit(solution)/shard_map/ppermute | solution.py:432
  13.6 3.3 %collective-permute-start.2 = (bf16[64,1024]{1,0:T(8,128)(2,1)S(1)}, bf16[64,1024]{1,0:T(8,128)(2,1)S(1)}, u32[]{:S(2)}, u32[]{:S(2)}) collective-permute-start(bf16[64,1024]{1,0:T(8,128)(2,1)S(1)} %copy-done.2), channel_id=1, source_target_pairs={{28,24},{29,25},{30,26},{31,27},{60,56},{61,57},{62,58},{63,59},{9... | collective-permute-start | bytes 393224 | tf_op jit(solution)/shard_map/ppermute | solution.py:448
  14.3 7.5 %collective-permute-start.3 = (bf16[64,1024]{1,0:T(8,128)(2,1)S(1)}, bf16[64,1024]{1,0:T(8,128)(2,1)S(1)}, u32[]{:S(2)}, u32[]{:S(2)}) collective-permute-start(bf16[64,1024]{1,0:T(8,128)(2,1)S(1)} %copy-done.2), channel_id=1, source_target_pairs={{8,0},{12,4},{16,8},{20,12},{24,16},{28,20},{4,28},{9,1},{13,5},{1... | collective-permute-start | bytes 393224 | tf_op jit(solution)/shard_map/ppermute | solution.py:410
  15.6 9.8 %collective-permute-start.4 = (bf16[64,1024]{1,0:T(8,128)(2,1)S(1)}, bf16[64,1024]{1,0:T(8,128)(2,1)S(1)}, u32[]{:S(2)}, u32[]{:S(2)}) collective-permute-start(bf16[64,1024]{1,0:T(8,128)(2,1)S(1)} %copy-done.2), channel_id=1, source_target_pairs={{24,0},{28,4},{20,28},{25,1},{29,5},{21,29},{26,2},{30,6},{22,30},... | collective-permute-start | bytes 393224 | tf_op jit(solution)/shard_map/ppermute | solution.py:410
  16.9 9.8 %collective-permute-start.5 = (bf16[64,1024]{1,0:T(8,128)(2,1)S(1)}, bf16[64,1024]{1,0:T(8,128)(2,1)S(1)}, u32[]{:S(2)}, u32[]{:S(2)}) collective-permute-start(bf16[64,1024]{1,0:T(8,128)(2,1)S(1)} %copy-done.2), channel_id=1, source_target_pairs={{16,0},{20,4},{24,8},{28,12},{12,28},{17,1},{21,5},{25,9},{29,13},... | collective-permute-start | bytes 393224 | tf_op jit(solution)/shard_map/ppermute | solution.py:410
  26.9 7.0 %collective-permute-start.9 = (bf16[256,1024]{1,0:T(8,128)(2,1)S(1)}, bf16[256,1024]{1,0:T(8,128)(2,1)S(1)}, u32[]{:S(2)}, u32[]{:S(2)}) collective-permute-start(bf16[256,1024]{1,0:T(8,128)(2,1)S(1)} %collective-permute-done.1.refs_11_), channel_id=1, source_target_pairs={{0,1},{1,0},{2,3},{3,2},{4,5},{5,4},{6,7},{7,6},{8,9},{9,8},{10,11... | collective-permute-start | bytes 1572872 | tf_op jit(solution)/shard_map/ppermute | solution.py:401
  32.4 3.2 %collective-permute-start.7 = (bf16[256,1024]{1,0:T(8,128)(2,1)}, bf16[256,1024]{1,0:T(8,128)(2,1)S(1)}, u32[]{:S(2)}, u32[]{:S(2)}) collective-permute-start(bf16[256,1024]{1,0:T(8,128)(2,1)} %shard_map.82.refs_7_), channel_id=1, source_target_pairs={{0,1},{1,0},{2,3},{3,2},{4,5},{5,4},{6,7},{7,6},{8,9},{9,8},{10,11... | collective-permute-start | bytes 1572872 | tf_op jit(solution)/shard_map/ppermute | solution.py:401
  32.5 3.1 %collective-permute-start.8 = (bf16[256,1024]{1,0:T(8,128)(2,1)S(1)}, bf16[256,1024]{1,0:T(8,128)(2,1)S(1)}, u32[]{:S(2)}, u32[]{:S(2)}) collective-permute-start(bf16[256,1024]{1,0:T(8,128)(2,1)S(1)} %collective-permute-done.refs_9_), channel_id=1, source_target_pairs={{0,1},{1,0},{2,3},{3,2},{4,5},{5,4},{6,7},{7,6},{8,9},{9,8},{10,11... | collective-permute-start | bytes 1572872 | tf_op jit(solution)/shard_map/ppermute | solution.py:401
  32.9 32.4 %collective-permute-start.6 = (bf16[256,1024]{1,0:T(8,128)(2,1)S(1)}, bf16[256,1024]{1,0:T(8,128)(2,1)S(1)}, u32[]{:S(2)}, u32[]{:S(2)}) collective-permute-start(bf16[256,1024]{1,0:T(8,128)(2,1)S(1)} %collective-permute-done.1.refs_11_), channel_id=1, source_target_pairs={{0,2},{2,0},{1,3},{3,1},{4,6},{6,4},{5,7},{7,5},{8,10},{10,8},{9,1... | collective-permute-start | bytes 1572872 | tf_op jit(solution)/shard_map/ppermute | solution.py:401
  35.7 1.0 copy-start
  36.7 35.9 %copy-start.4 = (bf16[1024,256]{1,0:T(8,128)(2,1)S(1)}, bf16[1024,256]{1,0:T(8,128)(2,1)}, u32[]{:S(2)}) copy-start(bf16[1024,256]{1,0:T(8,128)(2,1)} %refs_9_) | copy-start | bytes 1572868
  65.4 8.8 %collective-permute-start.11 = (bf16[256,1024]{1,0:T(8,128)(2,1)S(1)}, bf16[256,1024]{1,0:T(8,128)(2,1)S(1)}, u32[]{:S(2)}, u32[]{:S(2)}) collective-permute-start(bf16[256,1024]{1,0:T(8,128)(2,1)S(1)} %collective-permute-done.6.refs_7_), channel_id=1, source_target_pairs={{0,1},{1,0},{2,3},{3,2},{4,5},{5,4},{6,7},{7,6},{8,9},{9,8},{10,11... | collective-permute-start | bytes 1572872 | tf_op jit(solution)/shard_map/ppermute | solution.py:401
  72.7 20.7 %collective-permute-start.10 = (bf16[1024,256]{1,0:T(8,128)(2,1)S(1)}, bf16[1024,256]{1,0:T(8,128)(2,1)S(1)}, u32[]{:S(2)}, u32[]{:S(2)}) collective-permute-start(bf16[1024,256]{1,0:T(8,128)(2,1)S(1)} %copy-done.4), channel_id=1, source_target_pairs={{0,2},{2,0},{1,3},{3,1},{4,6},{6,4},{5,7},{7,5},{8,10},{10,8},{9,1... | collective-permute-start | bytes 1572872 | tf_op jit(solution)/shard_map/ppermute | solution.py:401
  79.4 7.5 %collective-permute-start.12 = (bf16[64,1152]{1,0:T(8,128)(2,1)S(1)}, bf16[64,1152]{1,0:T(8,128)(2,1)S(1)}, u32[]{:S(2)}, u32[]{:S(2)}) collective-permute-start(bf16[64,1152]{1,0:T(8,128)(2,1)S(1)} %get-tuple-element.88), channel_id=1, source_target_pairs={{0,16},{4,20},{8,24},{12,28},{28,12},{1,17},{5,21},{9,25},{13,29},... | collective-permute-start | bytes 442376 | tf_op jit(solution)/shard_map/ppermute | solution.py:415
  80.7 10.4 %collective-permute-start.13 = (bf16[64,1152]{1,0:T(8,128)(2,1)S(1)}, bf16[64,1152]{1,0:T(8,128)(2,1)S(1)}, u32[]{:S(2)}, u32[]{:S(2)}) collective-permute-start(bf16[64,1152]{1,0:T(8,128)(2,1)S(1)} %get-tuple-element.89), channel_id=1, source_target_pairs={{0,8},{4,12},{8,16},{12,20},{16,24},{20,28},{28,4},{1,9},{5,13},{9... | collective-permute-start | bytes 442376 | tf_op jit(solution)/shard_map/ppermute | solution.py:415
  84.9 7.7 %collective-permute-start.14 = (bf16[64,1152]{1,0:T(8,128)(2,1)S(1)}, bf16[64,1152]{1,0:T(8,128)(2,1)S(1)}, u32[]{:S(2)}, u32[]{:S(2)}) collective-permute-start(bf16[64,1152]{1,0:T(8,128)(2,1)S(1)} %get-tuple-element.90), channel_id=1, source_target_pairs={{0,24},{4,28},{28,20},{1,25},{5,29},{29,21},{2,26},{6,30},{30,22},... | collective-permute-start | bytes 442376 | tf_op jit(solution)/shard_map/ppermute | solution.py:415
  86.2 6.4 %collective-permute-start.15 = (bf16[64,1152]{1,0:T(8,128)(2,1)S(1)}, bf16[64,1152]{1,0:T(8,128)(2,1)S(1)}, u32[]{:S(2)}, u32[]{:S(2)}) collective-permute-start(bf16[64,1152]{1,0:T(8,128)(2,1)S(1)} %get-tuple-element.89), channel_id=1, source_target_pairs={{24,28},{25,29},{26,30},{27,31},{56,60},{57,61},{58,62},{59,63},{8... | collective-permute-start | bytes 442376 | tf_op jit(solution)/shard_map/ppermute | solution.py:465
  93.4 8.2 %collective-permute-start.16 = (bf16[64,1024]{1,0:T(8,128)(2,1)S(1)}, bf16[64,1024]{1,0:T(8,128)(2,1)S(1)}, u32[]{:S(2)}, u32[]{:S(2)}) collective-permute-start(bf16[64,1024]{1,0:T(8,128)(2,1)S(1)} %shard_map.85.refs_1_), channel_id=1, source_target_pairs={{8,0},{12,4},{16,8},{20,12},{24,16},{28,20},{0,24},{4,28},{9,1},{1... | collective-permute-start | bytes 393224 | tf_op jit(solution)/shard_map/ppermute | solution.py:410
  99.5 6.7 %collective-permute-start.18 = (bf16[64,1024]{1,0:T(8,128)(2,1)S(1)}, bf16[64,1024]{1,0:T(8,128)(2,1)S(1)}, u32[]{:S(2)}, u32[]{:S(2)}) collective-permute-start(bf16[64,1024]{1,0:T(8,128)(2,1)S(1)} %shard_map.85.refs_1_), channel_id=1, source_target_pairs={{24,0},{28,4},{0,8},{4,12},{8,16},{12,20},{16,24},{20,28},{25,1},{... | collective-permute-start | bytes 393224 | tf_op jit(solution)/shard_map/ppermute | solution.py:410
  106.3 9.3 %collective-permute-start.19 = (bf16[128,1024]{1,0:T(8,128)(2,1)S(1)}, bf16[128,1024]{1,0:T(8,128)(2,1)S(1)}, u32[]{:S(2)}, u32[]{:S(2)}) collective-permute-start(bf16[128,1024]{1,0:T(8,128)(2,1)S(1)} %get-tuple-element.110), channel_id=1, source_target_pairs={{28,0},{0,4},{4,8},{8,12},{12,16},{16,20},{20,24},{24,28},{29,1},{... | collective-permute-start | bytes 786440 | tf_op jit(solution)/shard_map/ppermute | solution.py:410
  110.6 10.7 %collective-permute-start.21 = (bf16[1024,256]{1,0:T(8,128)(2,1)S(1)}, bf16[1024,256]{1,0:T(8,128)(2,1)S(1)}, u32[]{:S(2)}, u32[]{:S(2)}) collective-permute-start(bf16[1024,256]{1,0:T(8,128)(2,1)S(1)} %copy-done.4), channel_id=1, source_target_pairs={{0,1},{1,0},{2,3},{3,2},{4,5},{5,4},{6,7},{7,6},{8,9},{9,8},{10,11... | collective-permute-start | bytes 1572872 | tf_op jit(solution)/shard_map/ppermute | solution.py:401
  111.6 13.3 %collective-permute-start.22 = (bf16[1024,256]{1,0:T(8,128)(2,1)S(1)}, bf16[1024,256]{1,0:T(8,128)(2,1)S(1)}, u32[]{:S(2)}, u32[]{:S(2)}) collective-permute-start(bf16[1024,256]{1,0:T(8,128)(2,1)S(1)} %collective-permute-done.10.refs_11_), channel_id=1, source_target_pairs={{0,1},{1,0},{2,3},{3,2},{4,5},{5,4},{6,7},{7,6},{8,9},{9,8},{10,11... | collective-permute-start | bytes 1572872 | tf_op jit(solution)/shard_map/ppermute | solution.py:401
  111.6 9.7 %collective-permute-start.17 = (bf16[128,1024]{1,0:T(8,128)(2,1)S(1)}, bf16[128,1024]{1,0:T(8,128)(2,1)S(1)}, u32[]{:S(2)}, u32[]{:S(2)}) collective-permute-start(bf16[128,1024]{1,0:T(8,128)(2,1)S(1)} %get-tuple-element.111), channel_id=1, source_target_pairs={{4,0},{8,4},{12,8},{16,12},{20,16},{24,20},{28,24},{0,28},{5,1},{9... | collective-permute-start | bytes 786440 | tf_op jit(solution)/shard_map/ppermute | solution.py:410
  113.1 11.7 %collective-permute-start.20 = (bf16[64,1024]{1,0:T(8,128)(2,1)S(1)}, bf16[64,1024]{1,0:T(8,128)(2,1)S(1)}, u32[]{:S(2)}, u32[]{:S(2)}) collective-permute-start(bf16[64,1024]{1,0:T(8,128)(2,1)S(1)} %shard_map.85.refs_1_), channel_id=1, source_target_pairs={{16,0},{20,4},{24,8},{28,12},{0,16},{4,20},{8,24},{12,28},{17,1},{... | collective-permute-start | bytes 393224 | tf_op jit(solution)/shard_map/ppermute | solution.py:410
  126.7 9.9 %collective-permute-start.23 = (bf16[2,64,1024]{2,1,0:T(8,128)(2,1)S(1)}, bf16[2,64,1024]{2,1,0:T(8,128)(2,1)S(1)}, u32[]{:S(2)}, u32[]{:S(2)}) collective-permute-start(bf16[2,64,1024]{2,1,0:T(8,128)(2,1)S(1)} %get-tuple-element.94), channel_id=1, source_target_pairs={{0,32},{32,64},{64,96},{96,0},{1,33},{33,65},{65,97},{97,1},{2,34}... | collective-permute-start | bytes 786440 | tf_op jit(solution)/shard_map/ppermute | solution.py:480
  126.8 13.0 %collective-permute-start.24 = (bf16[2,64,1024]{2,1,0:T(8,128)(2,1)S(1)}, bf16[2,64,1024]{2,1,0:T(8,128)(2,1)S(1)}, u32[]{:S(2)}, u32[]{:S(2)}) collective-permute-start(bf16[2,64,1024]{2,1,0:T(8,128)(2,1)S(1)} %get-tuple-element.95), channel_id=1, source_target_pairs={{0,64},{32,96},{64,0},{96,32},{1,65},{33,97},{65,1},{97,33},{2,66}... | collective-permute-start | bytes 786440 | tf_op jit(solution)/shard_map/ppermute | solution.py:480
  129.1 12.3 %collective-permute-start.25 = (bf16[2,64,1024]{2,1,0:T(8,128)(2,1)S(1)}, bf16[2,64,1024]{2,1,0:T(8,128)(2,1)S(1)}, u32[]{:S(2)}, u32[]{:S(2)}) collective-permute-start(bf16[2,64,1024]{2,1,0:T(8,128)(2,1)S(1)} %get-tuple-element.96), channel_id=1, source_target_pairs={{0,96},{32,0},{64,32},{96,64},{1,97},{33,1},{65,33},{97,65},{2,98}... | collective-permute-start | bytes 786440 | tf_op jit(solution)/shard_map/ppermute | solution.py:480
  141.6 3.9 %collective-permute-start.26 = (bf16[64,512]{1,0:T(8,128)(2,1)S(1)}, bf16[64,512]{1,0:T(8,128)(2,1)S(1)}, u32[]{:S(2)}, u32[]{:S(2)}) collective-permute-start(bf16[64,512]{1,0:T(8,128)(2,1)S(1)} %get-tuple-element.101), channel_id=1, source_target_pairs={{0,128},{2,130},{128,0},{130,2},{1,129},{3,131},{129,1},{131,3},{4... | collective-permute-start | bytes 196616 | tf_op jit(solution)/shard_map/ppermute | solution.py:489
  141.7 4.7 %collective-permute-start.27 = (bf16[64,512]{1,0:T(8,128)(2,1)S(1)}, bf16[64,512]{1,0:T(8,128)(2,1)S(1)}, u32[]{:S(2)}, u32[]{:S(2)}) collective-permute-start(bf16[64,512]{1,0:T(8,128)(2,1)S(1)} %get-tuple-element.103), channel_id=1, source_target_pairs={{0,2},{2,0},{128,130},{130,128},{1,3},{3,1},{129,131},{131,129},{4... | collective-permute-start | bytes 196616 | tf_op jit(solution)/shard_map/ppermute | solution.py:489
  141.8 5.7 %collective-permute-start.28 = (bf16[64,512]{1,0:T(8,128)(2,1)S(1)}, bf16[64,512]{1,0:T(8,128)(2,1)S(1)}, u32[]{:S(2)}, u32[]{:S(2)}) collective-permute-start(bf16[64,512]{1,0:T(8,128)(2,1)S(1)} %get-tuple-element.102), channel_id=1, source_target_pairs={{0,130},{2,128},{128,2},{130,0},{1,131},{3,129},{129,3},{131,1},{4... | collective-permute-start | bytes 196616 | tf_op jit(solution)/shard_map/ppermute | solution.py:489
  147.5 3.7 %collective-permute-start.29 = (bf16[2,64,256]{2,1,0:T(8,128)(2,1)S(1)}, bf16[2,64,256]{2,1,0:T(8,128)(2,1)S(1)}, u32[]{:S(2)}, u32[]{:S(2)}) collective-permute-start(bf16[2,64,256]{2,1,0:T(8,128)(2,1)S(1)} %pad_maximum_fusion.3), channel_id=1, source_target_pairs={{0,1},{1,0},{2,3},{3,2},{4,5},{5,4},{6,7},{7,6},{8,9},{9,8},{10,11... | collective-permute-start | bytes 196616 | tf_op jit(solution)/shard_map/ppermute | solution.py:401

commit v3 on v1

--- a/solution.py
+++ b/solution.py
@@ -21,7 +21,7 @@
 SMEM = pl.BlockSpec(memory_space=pltpu.SMEM)
 ANY = pl.BlockSpec(memory_space=pl.ANY)
 LIMIT = 24 * 1024 * 1024
-FLASH_LIMIT = 40 * 1024 * 1024
+FLASH_LIMIT = 28 * 1024 * 1024
 REBUILD_LIMIT = 60 * 1024 * 1024
 SHIFTS = (0, 2, 6, 4)
 

time: 153 us -> 152 us (level); the launches traced: 154 us -> 155 us
  Pallas kernels: 42.2 us -> 46 us
  waiting for transfers between devices: 51.4 us -> 49.1 us
    pallas_call x2, Pallas kernels: 37.4 us -> 41.2 us  [flash(): pl.pallas_call(functools.partial(flash_kernel, nq, nk, first, last, group...]
    ppermute x3, waiting for transfers between devices: 4.84 us -> 1.65 us  [along_y(): return lax.ppermute(array, ('yl', 'yh'), pairs)]
    ppermute x10, starting transfers between devices: 18.7 us -> 21.4 us  [fetch(): return lax.ppermute(array, 'z', pairs)]
    ppermute x3, waiting for transfers between devices: 6.4 us -> 8.54 us  [give(): return lax.ppermute(array, 'z', pairs)]
    ppermute x3, starting transfers between devices: 7.28 us -> 5.23 us  [give(): return lax.ppermute(array, 'z', pairs)]
  transfers between devices with their start and end apart: 32 -> 32, of which waited for: 16 -> 16; matrix products, arithmetic and copies ran while one was open for 0% -> 0% of each run, Pallas kernels for 25% -> 27%
where the time goes in v3:
time: 152 us; the launch traced here: 155 us
  starting transfers between devices  57.3 us (38%)
  waiting for transfers between devices  49.1 us (32%)
  Pallas kernels  46 us (30%)
  local copies, waits for them, and re-layouts  1.82 us (1%)
    pallas_call x2, Pallas kernels, flash(): pl.pallas_call(functools.partial(flash_kernel, nq, nk, first, last, group...  41.2 us
    ppermute x10, waiting for transfers between devices, fetch(): return lax.ppermute(array, 'z', pairs)  24.7 us
    ppermute x10, starting transfers between devices, fetch(): return lax.ppermute(array, 'z', pairs)  21.4 us
    ppermute x10, starting transfers between devices, swap(): return lax.ppermute(array, axis, [(0, 1), (1, 0)])  11.9 us
    ppermute x3, waiting for transfers between devices, along_x(): return lax.ppermute(array, 'x', [(n, (n + k) % 4) for n in range(4)])  10.6 us
    ppermute x3, waiting for transfers between devices, give(): return lax.ppermute(array, 'z', pairs)  8.54 us
    ppermute x1, starting transfers between devices, beside(): return lax.ppermute(array, ('z', 'yh', 'core'), pairs)  7.5 us
    ppermute x3, starting transfers between devices, along_x(): return lax.ppermute(array, 'x', [(n, (n + k) % 4) for n in range(4)])  6.01 us
  transfers between devices with their start and end apart: 32, of which 16 were waited for; matrix products, arithmetic and copies ran while one was open for 0% of the time, Pallas kernels for 27%

profile of v3, /device:TPU:1, one launch (start us, length us, event | category | flops | bytes accessed | tf_op | source)
XLA Modules:
  0.0 154.6 jit_solution(7668208793640200224)
XLA Ops:
  0.0 2.2 %shard_map.82.refs_7_ = bf16[256,1024]{1,0:T(8,128)(2,1)} custom-call(bf16[1024,128]{1,0:T(8,128)(2,1)} %lk_in.1, bf16[1024,128]{1,0:T(8,128)(2,1)} %lv_in.1, bf16[1,128,128]{2,1,0:T(8,128)(2,1)} %bk_in.1, bf16[1,128,128]{2,1,0:T(8,128)(2,1)} %bv_in.1), custom_call_target="tpu_custom_call" | custom-call | flops 67108864 | bytes 1048576 | tf_op jit(solution)/shard_map/pallas_call | solution.py:54
  2.2 3.8 %collective-permute-start.3 = (bf16[256,1024]{1,0:T(8,128)(2,1)}, bf16[256,1024]{1,0:T(8,128)(2,1)S(1)}, u32[]{:S(2)}, u32[]{:S(2)}) collective-permute-start(bf16[256,1024]{1,0:T(8,128)(2,1)} %shard_map.82.refs_7_), channel_id=1, source_target_pairs={{0,2},{2,0},{1,3},{3,1},{4,6},{6,4},{5,7},{7,5},{8,10},{10,8},{9,1... | collective-permute-start | bytes 1572872 | tf_op jit(solution)/shard_map/ppermute | solution.py:403
  6.1 7.5 %collective-permute-start.4 = (bf16[256,1024]{1,0:T(8,128)(2,1)}, bf16[256,1024]{1,0:T(8,128)(2,1)S(1)}, u32[]{:S(2)}, u32[]{:S(2)}) collective-permute-start(bf16[256,1024]{1,0:T(8,128)(2,1)} %shard_map.82.refs_7_), channel_id=1, source_target_pairs={{4,0},{6,2},{8,4},{10,6},{12,8},{5,9},{14,10},{7,11},{16,12},{9,13... | collective-permute-start | bytes 1572872 | tf_op jit(solution)/shard_map/ppermute | solution.py:434
  13.6 1.3 collective-permute-start
  14.9 1.3 collective-permute-start.1
  16.2 1.3 collective-permute-start.2
  17.5 6.8 %collective-permute-done.refs_5_ = bf16[64,1024]{1,0:T(8,128)(2,1)S(1)} collective-permute-done((bf16[64,1024]{1,0:T(8,128)(2,1)S(1)}, bf16[64,1024]{1,0:T(8,128)(2,1)S(1)}, u32[]{:S(2)}, u32[]{:S(2)}) %collective-permute-start) | collective-permute-done | bytes 131104 | tf_op jit(solution)/shard_map/ppermute | solution.py:412
  24.3 0.7 collective-permute-start.5
  25.0 3.9 %collective-permute-done.1.refs_3_ = bf16[64,1024]{1,0:T(8,128)(2,1)S(1)} collective-permute-done((bf16[64,1024]{1,0:T(8,128)(2,1)S(1)}, bf16[64,1024]{1,0:T(8,128)(2,1)S(1)}, u32[]{:S(2)}, u32[]{:S(2)}) %collective-permute-start.1) | collective-permute-done | bytes 131104 | tf_op jit(solution)/shard_map/ppermute | solution.py:412
  28.9 1.2 collective-permute-done.2.refs_4_
  30.0 1.8 %collective-permute-start.9 = (bf16[256,1024]{1,0:T(8,128)(2,1)S(1)}, bf16[256,1024]{1,0:T(8,128)(2,1)S(1)}, u32[]{:S(2)}, u32[]{:S(2)}) collective-permute-start(bf16[256,1024]{1,0:T(8,128)(2,1)S(1)} %collective-permute-done.4.refs_11_), channel_id=1, source_target_pairs={{0,1},{1,0},{2,3},{3,2},{4,5},{5,4},{6,7},{7,6},{8,9},{9,8},{10,11... | collective-permute-start | bytes 1572872 | tf_op jit(solution)/shard_map/ppermute | solution.py:403
  31.8 0.1 collective-permute-start.7
  31.9 0.4 collective-permute-start.8
  32.4 1.0 collective-permute-done.9.refs_12_
  33.4 1.7 %collective-permute-done.7.refs_8_ = bf16[256,1024]{1,0:T(8,128)(2,1)S(1)} collective-permute-done((bf16[256,1024]{1,0:T(8,128)(2,1)}, bf16[256,1024]{1,0:T(8,128)(2,1)S(1)}, u32[]{:S(2)}, u32[]{:S(2)}) %collective-permute-start.7) | collective-permute-done | bytes 524320 | tf_op jit(solution)/shard_map/ppermute | solution.py:403
  35.1 1.0 copy-done
  36.1 32.2 %shard_map.83 = (f32[8,512]{1,0:T(8,128)S(1)}, f32[8,512]{1,0:T(8,128)S(1)}, f32[128,512]{1,0:T(8,128)S(1)}, f32[8,512]{1,0:T(8,128)S(1)}, f32[8,512]{1,0:T(8,12...) custom-call(s32[256,128]{1,0:T(8,128)S(1)} %bitcast.35, ...), custom_call_target="tpu_custom_call" | custom-call | flops 1000000 | bytes 100000 | tf_op jit(solution)/shard_map/pallas_call | solution.py:320
  68.4 0.1 collective-permute-start.11
  68.5 1.9 %collective-permute-start.10 = (bf16[1024,256]{1,0:T(8,128)(2,1)S(1)}, bf16[1024,256]{1,0:T(8,128)(2,1)S(1)}, u32[]{:S(2)}, u32[]{:S(2)}) collective-permute-start(bf16[1024,256]{1,0:T(8,128)(2,1)S(1)} %copy-done.4), channel_id=1, source_target_pairs={{0,2},{2,0},{1,3},{3,1},{4,6},{6,4},{5,7},{7,5},{8,10},{10,8},{9,1... | collective-permute-start | bytes 1572872 | tf_op jit(solution)/shard_map/ppermute | solution.py:403
  70.4 8.9 %shard_map.84 = (bf16[64,1152]{1,0:T(8,128)(2,1)S(1)}, bf16[64,1152]{1,0:T(8,128)(2,1)S(1)}, bf16[64,1152]{1,0:T(8,128)(2,1)S(1)}, bf16[64,1152]{1,0:T(8,128)(2,1)S(1)}) custom-call(s32[256,128]{1,0:T(8,128)S(1)} %bitcast.36, s32[16,128]{1,0:T(8,128)S(1)} %bitcast.38, bf16[64,1024]{1,0:T(8,128)(2,1)S(1)} %copy-done.2, ...), custom_call_target="tpu_custom_call" | custom-call | flops 1000000 | bytes 100000 | tf_op jit(solution)/shard_map/pallas_call | solution.py:320
  79.3 1.3 collective-permute-start.12
  80.6 2.6 %collective-permute-start.13 = (bf16[64,1152]{1,0:T(8,128)(2,1)S(1)}, bf16[64,1152]{1,0:T(8,128)(2,1)S(1)}, u32[]{:S(2)}, u32[]{:S(2)}) collective-permute-start(bf16[64,1152]{1,0:T(8,128)(2,1)S(1)} %get-tuple-element.83), channel_id=1, source_target_pairs={{0,8},{4,12},{8,16},{12,20},{16,24},{20,28},{28,4},{1,9},{5,13},{9... | collective-permute-start | bytes 442376 | tf_op jit(solution)/shard_map/ppermute | solution.py:417
  83.3 1.3 collective-permute-start.14
  84.6 0.7 collective-permute-start.15
  85.3 0.1 collective-permute-start.23
  85.4 1.7 %collective-permute-done.13.refs_2_ = bf16[64,1152]{1,0:T(8,128)(2,1)S(1)} collective-permute-done((bf16[64,1152]{1,0:T(8,128)(2,1)S(1)}, bf16[64,1152]{1,0:T(8,128)(2,1)S(1)}, u32[]{:S(2)}, u32[]{:S(2)}) %collective-permute-start.13) | collective-permute-done | bytes 147488 | tf_op jit(solution)/shard_map/ppermute | solution.py:417
  87.0 6.9 %collective-permute-done.14.refs_3_ = bf16[64,1152]{1,0:T(8,128)(2,1)S(1)} collective-permute-done((bf16[64,1152]{1,0:T(8,128)(2,1)S(1)}, bf16[64,1152]{1,0:T(8,128)(2,1)S(1)}, u32[]{:S(2)}, u32[]{:S(2)}) %collective-permute-start.14) | collective-permute-done | bytes 147488 | tf_op jit(solution)/shard_map/ppermute | solution.py:417
  93.9 0.7 shard_map.85.refs_1_
  94.8 8.8 %collective-permute-start.18 = (bf16[64,1024]{1,0:T(8,128)(2,1)S(1)}, bf16[64,1024]{1,0:T(8,128)(2,1)S(1)}, u32[]{:S(2)}, u32[]{:S(2)}) collective-permute-start(bf16[64,1024]{1,0:T(8,128)(2,1)S(1)} %shard_map.85.refs_1_), channel_id=1, source_target_pairs={{8,0},{12,4},{16,8},{20,12},{24,16},{28,20},{0,24},{4,28},{9,1},{1... | collective-permute-start | bytes 393224 | tf_op jit(solution)/shard_map/ppermute | solution.py:412
  103.6 4.6 %collective-permute-start.16 = (bf16[64,1024]{1,0:T(8,128)(2,1)S(1)}, bf16[64,1024]{1,0:T(8,128)(2,1)S(1)}, u32[]{:S(2)}, u32[]{:S(2)}) collective-permute-start(bf16[64,1024]{1,0:T(8,128)(2,1)S(1)} %shard_map.85.refs_1_), channel_id=1, source_target_pairs={{4,0},{8,4},{12,8},{16,12},{20,16},{24,20},{28,24},{0,28},{5,1},{9... | collective-permute-start | bytes 393224 | tf_op jit(solution)/shard_map/ppermute | solution.py:412
  108.2 2.6 %collective-permute-start.20 = (bf16[64,1024]{1,0:T(8,128)(2,1)S(1)}, bf16[64,1024]{1,0:T(8,128)(2,1)S(1)}, u32[]{:S(2)}, u32[]{:S(2)}) collective-permute-start(bf16[64,1024]{1,0:T(8,128)(2,1)S(1)} %shard_map.85.refs_1_), channel_id=1, source_target_pairs={{16,0},{20,4},{24,8},{28,12},{0,16},{4,20},{8,24},{12,28},{17,1},{... | collective-permute-start | bytes 393224 | tf_op jit(solution)/shard_map/ppermute | solution.py:412
  110.8 3.0 %collective-permute-done.19.refs_5_ = bf16[64,1024]{1,0:T(8,128)(2,1)S(1)} collective-permute-done((bf16[64,1024]{1,0:T(8,128)(2,1)S(1)}, bf16[64,1024]{1,0:T(8,128)(2,1)S(1)}, u32[]{:S(2)}, u32[]{:S(2)}) %collective-permute-start.19) | collective-permute-done | bytes 131104 | tf_op jit(solution)/shard_map/ppermute | solution.py:412
  113.9 1.5 collective-permute-start.22
  115.4 3.9 %collective-permute-done.17.refs_3_ = bf16[64,1024]{1,0:T(8,128)(2,1)S(1)} collective-permute-done((bf16[64,1024]{1,0:T(8,128)(2,1)S(1)}, bf16[64,1024]{1,0:T(8,128)(2,1)S(1)}, u32[]{:S(2)}, u32[]{:S(2)}) %collective-permute-start.17) | collective-permute-done | bytes 131104 | tf_op jit(solution)/shard_map/ppermute | solution.py:412
  119.3 2.6 %collective-permute-done.21.refs_7_ = bf16[64,1024]{1,0:T(8,128)(2,1)S(1)} collective-permute-done((bf16[64,1024]{1,0:T(8,128)(2,1)S(1)}, bf16[64,1024]{1,0:T(8,128)(2,1)S(1)}, u32[]{:S(2)}, u32[]{:S(2)}) %collective-permute-start.21) | collective-permute-done | bytes 131104 | tf_op jit(solution)/shard_map/ppermute | solution.py:412
  122.0 3.2 %collective-permute-done.22.refs_8_ = bf16[64,1024]{1,0:T(8,128)(2,1)S(1)} collective-permute-done((bf16[64,1024]{1,0:T(8,128)(2,1)S(1)}, bf16[64,1024]{1,0:T(8,128)(2,1)S(1)}, u32[]{:S(2)}, u32[]{:S(2)}) %collective-permute-start.22) | collective-permute-done | bytes 131104 | tf_op jit(solution)/shard_map/ppermute | solution.py:412
  125.2 1.9 %shard_map.86 = (bf16[2,64,1024]{2,1,0:T(8,128)(2,1)S(1)}, bf16[2,64,1024]{2,1,0:T(8,128)(2,1)S(1)}, bf16[2,64,1024]{2,1,0:T(8,128)(2,1)S(1)}, bf16[2,64,1024]{2,1,0:T(8,128)(2,1)S(1)}) custom-call(s32[8]{0:T(128)S(1)} %stack.53.refs_0_, bf16[64,1024]{1,0:T(8,128)(2,1)S(1)} %shard_map.85.refs_1_, bf16[64,1024]{1,0:T(8,128)(2,1)S(1)} %collective-permute-done.16.refs_2_, ...), custom_call_target="tpu_custom_call" | custom-call | flops 1073741824 | bytes 4000000 | tf_op jit(solution)/shard_map/pallas_call | solution.py:391
  127.1 5.7 %collective-permute-start.26 = (bf16[2,64,1024]{2,1,0:T(8,128)(2,1)S(1)}, bf16[2,64,1024]{2,1,0:T(8,128)(2,1)S(1)}, u32[]{:S(2)}, u32[]{:S(2)}) collective-permute-start(bf16[2,64,1024]{2,1,0:T(8,128)(2,1)S(1)} %get-tuple-element.89), channel_id=1, source_target_pairs={{0,64},{32,96},{64,0},{96,32},{1,65},{33,97},{65,1},{97,33},{2,66}... | collective-permute-start | bytes 786440 | tf_op jit(solution)/shard_map/ppermute | solution.py:484
  132.8 0.3 collective-permute-start.27
  133.0 4.1 %collective-permute-done.25 = bf16[2,64,1024]{2,1,0:T(8,128)(2,1)S(1)} collective-permute-done((bf16[2,64,1024]{2,1,0:T(8,128)(2,1)S(1)}, bf16[2,64,1024]{2,1,0:T(8,128)(2,1)S(1)}, u32[]{:S(2)}, u32[]{:S(2)}) %collective-permute-start.25) | collective-permute-done | bytes 262176 | tf_op jit(solution)/shard_map/ppermute | solution.py:484
  137.1 6.5 %collective-permute-done.26 = bf16[2,64,1024]{2,1,0:T(8,128)(2,1)S(1)} collective-permute-done((bf16[2,64,1024]{2,1,0:T(8,128)(2,1)S(1)}, bf16[2,64,1024]{2,1,0:T(8,128)(2,1)S(1)}, u32[]{:S(2)}, u32[]{:S(2)}) %collective-permute-start.26) | collective-permute-done | bytes 262176 | tf_op jit(solution)/shard_map/ppermute | solution.py:484
  143.6 0.2 fusion.3
  144.0 3.7 %collective-permute-start.30 = (bf16[64,512]{1,0:T(8,128)(2,1)S(1)}, bf16[64,512]{1,0:T(8,128)(2,1)S(1)}, u32[]{:S(2)}, u32[]{:S(2)}) collective-permute-start(bf16[64,512]{1,0:T(8,128)(2,1)S(1)} %get-tuple-element.96), channel_id=1, source_target_pairs={{0,130},{2,128},{128,2},{130,0},{1,131},{3,129},{129,3},{131,1},{4... | collective-permute-start | bytes 196616 | tf_op jit(solution)/shard_map/ppermute | solution.py:493
  147.8 0.9 collective-permute-done.29
  148.7 0.8 collective-permute-done.30
  149.5 3.5 %collective-permute-start.31 = (bf16[2,64,256]{2,1,0:T(8,128)(2,1)S(1)}, bf16[2,64,256]{2,1,0:T(8,128)(2,1)S(1)}, u32[]{:S(2)}, u32[]{:S(2)}) collective-permute-start(bf16[2,64,256]{2,1,0:T(8,128)(2,1)S(1)} %pad_maximum_fusion.1), channel_id=1, source_target_pairs={{0,1},{1,0},{2,3},{3,2},{4,5},{5,4},{6,7},{7,6},{8,9},{9,8},{10,11... | collective-permute-start | bytes 196616 | tf_op jit(solution)/shard_map/ppermute | solution.py:403
  153.0 0.9 collective-permute-done.31
  154.0 0.7 copy.9
  (39 shorter events, 0.7 us)
Async XLA Ops:
  0.0 13.6 %copy-start.2 = (bf16[64,1024]{1,0:T(8,128)(2,1)S(1)}, bf16[64,1024]{1,0:T(8,128)(2,1)}, u32[]{:S(2)}) copy-start(bf16[64,1024]{1,0:T(8,128)(2,1)} %refs_2_.3) | copy-start | bytes 393220
  0.0 35.1 %copy-start.1 = (s32[32768]{0:T(1024)S(1)}, s32[32768]{0:T(1024)}, u32[]{:S(2)}) copy-start(s32[32768]{0:T(1024)} %param.15) | copy-start | bytes 393220
  0.0 35.1 %copy-start.3 = (s32[2048]{0:T(1024)S(1)}, s32[2048]{0:T(1024)}, u32[]{:S(2)}) copy-start(s32[2048]{0:T(1024)} %param.14) | copy-start | bytes 24580
  2.2 27.8 %collective-permute-start.3 = (bf16[256,1024]{1,0:T(8,128)(2,1)}, bf16[256,1024]{1,0:T(8,128)(2,1)S(1)}, u32[]{:S(2)}, u32[]{:S(2)}) collective-permute-start(bf16[256,1024]{1,0:T(8,128)(2,1)} %shard_map.82.refs_7_), channel_id=1, source_target_pairs={{0,2},{2,0},{1,3},{3,1},{4,6},{6,4},{5,7},{7,5},{8,10},{10,8},{9,1... | collective-permute-start | bytes 1572872 | tf_op jit(solution)/shard_map/ppermute | solution.py:403
  6.1 24.0 %collective-permute-start.4 = (bf16[256,1024]{1,0:T(8,128)(2,1)}, bf16[256,1024]{1,0:T(8,128)(2,1)S(1)}, u32[]{:S(2)}, u32[]{:S(2)}) collective-permute-start(bf16[256,1024]{1,0:T(8,128)(2,1)} %shard_map.82.refs_7_), channel_id=1, source_target_pairs={{4,0},{6,2},{8,4},{10,6},{12,8},{5,9},{14,10},{7,11},{16,12},{9,13... | collective-permute-start | bytes 1572872 | tf_op jit(solution)/shard_map/ppermute | solution.py:434
  13.6 10.7 %collective-permute-start = (bf16[64,1024]{1,0:T(8,128)(2,1)S(1)}, bf16[64,1024]{1,0:T(8,128)(2,1)S(1)}, u32[]{:S(2)}, u32[]{:S(2)}) collective-permute-start(bf16[64,1024]{1,0:T(8,128)(2,1)S(1)} %copy-done.2), channel_id=1, source_target_pairs={{16,0},{20,4},{24,8},{28,12},{12,28},{17,1},{21,5},{25,9},{29,13},... | collective-permute-start | bytes 393224 | tf_op jit(solution)/shard_map/ppermute | solution.py:412
  14.9 14.0 %collective-permute-start.1 = (bf16[64,1024]{1,0:T(8,128)(2,1)S(1)}, bf16[64,1024]{1,0:T(8,128)(2,1)S(1)}, u32[]{:S(2)}, u32[]{:S(2)}) collective-permute-start(bf16[64,1024]{1,0:T(8,128)(2,1)S(1)} %copy-done.2), channel_id=1, source_target_pairs={{8,0},{12,4},{16,8},{20,12},{24,16},{28,20},{4,28},{9,1},{13,5},{1... | collective-permute-start | bytes 393224 | tf_op jit(solution)/shard_map/ppermute | solution.py:412
  16.2 13.8 %collective-permute-start.2 = (bf16[64,1024]{1,0:T(8,128)(2,1)S(1)}, bf16[64,1024]{1,0:T(8,128)(2,1)S(1)}, u32[]{:S(2)}, u32[]{:S(2)}) collective-permute-start(bf16[64,1024]{1,0:T(8,128)(2,1)S(1)} %copy-done.2), channel_id=1, source_target_pairs={{24,0},{28,4},{20,28},{25,1},{29,5},{21,29},{26,2},{30,6},{22,30},... | collective-permute-start | bytes 393224 | tf_op jit(solution)/shard_map/ppermute | solution.py:412
  24.3 5.7 %collective-permute-start.5 = (bf16[64,1024]{1,0:T(8,128)(2,1)S(1)}, bf16[64,1024]{1,0:T(8,128)(2,1)S(1)}, u32[]{:S(2)}, u32[]{:S(2)}) collective-permute-start(bf16[64,1024]{1,0:T(8,128)(2,1)S(1)} %copy-done.2), channel_id=1, source_target_pairs={{28,24},{29,25},{30,26},{31,27},{60,56},{61,57},{62,58},{63,59},{9... | collective-permute-start | bytes 393224 | tf_op jit(solution)/shard_map/ppermute | solution.py:450
  30.0 3.3 %collective-permute-start.9 = (bf16[256,1024]{1,0:T(8,128)(2,1)S(1)}, bf16[256,1024]{1,0:T(8,128)(2,1)S(1)}, u32[]{:S(2)}, u32[]{:S(2)}) collective-permute-start(bf16[256,1024]{1,0:T(8,128)(2,1)S(1)} %collective-permute-done.4.refs_11_), channel_id=1, source_target_pairs={{0,1},{1,0},{2,3},{3,2},{4,5},{5,4},{6,7},{7,6},{8,9},{9,8},{10,11... | collective-permute-start | bytes 1572872 | tf_op jit(solution)/shard_map/ppermute | solution.py:403
  31.8 3.2 %collective-permute-start.7 = (bf16[256,1024]{1,0:T(8,128)(2,1)}, bf16[256,1024]{1,0:T(8,128)(2,1)S(1)}, u32[]{:S(2)}, u32[]{:S(2)}) collective-permute-start(bf16[256,1024]{1,0:T(8,128)(2,1)} %shard_map.82.refs_7_), channel_id=1, source_target_pairs={{0,1},{1,0},{2,3},{3,2},{4,5},{5,4},{6,7},{7,6},{8,9},{9,8},{10,11... | collective-permute-start | bytes 1572872 | tf_op jit(solution)/shard_map/ppermute | solution.py:403
  31.9 3.1 %collective-permute-start.8 = (bf16[256,1024]{1,0:T(8,128)(2,1)S(1)}, bf16[256,1024]{1,0:T(8,128)(2,1)S(1)}, u32[]{:S(2)}, u32[]{:S(2)}) collective-permute-start(bf16[256,1024]{1,0:T(8,128)(2,1)S(1)} %collective-permute-done.3.refs_9_), channel_id=1, source_target_pairs={{0,1},{1,0},{2,3},{3,2},{4,5},{5,4},{6,7},{7,6},{8,9},{9,8},{10,11... | collective-permute-start | bytes 1572872 | tf_op jit(solution)/shard_map/ppermute | solution.py:403
  32.3 36.0 %collective-permute-start.6 = (bf16[256,1024]{1,0:T(8,128)(2,1)S(1)}, bf16[256,1024]{1,0:T(8,128)(2,1)S(1)}, u32[]{:S(2)}, u32[]{:S(2)}) collective-permute-start(bf16[256,1024]{1,0:T(8,128)(2,1)S(1)} %collective-permute-done.4.refs_11_), channel_id=1, source_target_pairs={{0,2},{2,0},{1,3},{3,1},{4,6},{6,4},{5,7},{7,5},{8,10},{10,8},{9,1... | collective-permute-start | bytes 1572872 | tf_op jit(solution)/shard_map/ppermute | solution.py:403
  35.1 1.0 copy-start
  36.1 32.4 %copy-start.4 = (bf16[1024,256]{1,0:T(8,128)(2,1)S(1)}, bf16[1024,256]{1,0:T(8,128)(2,1)}, u32[]{:S(2)}) copy-start(bf16[1024,256]{1,0:T(8,128)(2,1)} %refs_9_) | copy-start | bytes 1572868
  68.4 2.0 %collective-permute-start.11 = (bf16[256,1024]{1,0:T(8,128)(2,1)S(1)}, bf16[256,1024]{1,0:T(8,128)(2,1)S(1)}, u32[]{:S(2)}, u32[]{:S(2)}) collective-permute-start(bf16[256,1024]{1,0:T(8,128)(2,1)S(1)} %collective-permute-done.6.refs_7_), channel_id=1, source_target_pairs={{0,1},{1,0},{2,3},{3,2},{4,5},{5,4},{6,7},{7,6},{8,9},{9,8},{10,11... | collective-permute-start | bytes 1572872 | tf_op jit(solution)/shard_map/ppermute | solution.py:403
  68.5 26.2 %collective-permute-start.10 = (bf16[1024,256]{1,0:T(8,128)(2,1)S(1)}, bf16[1024,256]{1,0:T(8,128)(2,1)S(1)}, u32[]{:S(2)}, u32[]{:S(2)}) collective-permute-start(bf16[1024,256]{1,0:T(8,128)(2,1)S(1)} %copy-done.4), channel_id=1, source_target_pairs={{0,2},{2,0},{1,3},{3,1},{4,6},{6,4},{5,7},{7,5},{8,10},{10,8},{9,1... | collective-permute-start | bytes 1572872 | tf_op jit(solution)/shard_map/ppermute | solution.py:403
  79.3 5.9 %collective-permute-start.12 = (bf16[64,1152]{1,0:T(8,128)(2,1)S(1)}, bf16[64,1152]{1,0:T(8,128)(2,1)S(1)}, u32[]{:S(2)}, u32[]{:S(2)}) collective-permute-start(bf16[64,1152]{1,0:T(8,128)(2,1)S(1)} %get-tuple-element.82), channel_id=1, source_target_pairs={{0,16},{4,20},{8,24},{12,28},{28,12},{1,17},{5,21},{9,25},{13,29},... | collective-permute-start | bytes 442376 | tf_op jit(solution)/shard_map/ppermute | solution.py:417
  80.6 6.4 %collective-permute-start.13 = (bf16[64,1152]{1,0:T(8,128)(2,1)S(1)}, bf16[64,1152]{1,0:T(8,128)(2,1)S(1)}, u32[]{:S(2)}, u32[]{:S(2)}) collective-permute-start(bf16[64,1152]{1,0:T(8,128)(2,1)S(1)} %get-tuple-element.83), channel_id=1, source_target_pairs={{0,8},{4,12},{8,16},{12,20},{16,24},{20,28},{28,4},{1,9},{5,13},{9... | collective-permute-start | bytes 442376 | tf_op jit(solution)/shard_map/ppermute | solution.py:417
  83.3 10.6 %collective-permute-start.14 = (bf16[64,1152]{1,0:T(8,128)(2,1)S(1)}, bf16[64,1152]{1,0:T(8,128)(2,1)S(1)}, u32[]{:S(2)}, u32[]{:S(2)}) collective-permute-start(bf16[64,1152]{1,0:T(8,128)(2,1)S(1)} %get-tuple-element.84), channel_id=1, source_target_pairs={{0,24},{4,28},{28,20},{1,25},{5,29},{29,21},{2,26},{6,30},{30,22},... | collective-permute-start | bytes 442376 | tf_op jit(solution)/shard_map/ppermute | solution.py:417
  84.6 9.3 %collective-permute-start.15 = (bf16[64,1152]{1,0:T(8,128)(2,1)S(1)}, bf16[64,1152]{1,0:T(8,128)(2,1)S(1)}, u32[]{:S(2)}, u32[]{:S(2)}) collective-permute-start(bf16[64,1152]{1,0:T(8,128)(2,1)S(1)} %get-tuple-element.83), channel_id=1, source_target_pairs={{24,28},{25,29},{26,30},{27,31},{56,60},{57,61},{58,62},{59,63},{8... | collective-permute-start | bytes 442376 | tf_op jit(solution)/shard_map/ppermute | solution.py:471
  85.3 22.9 %collective-permute-start.23 = (bf16[1024,256]{1,0:T(8,128)(2,1)S(1)}, bf16[1024,256]{1,0:T(8,128)(2,1)S(1)}, u32[]{:S(2)}, u32[]{:S(2)}) collective-permute-start(bf16[1024,256]{1,0:T(8,128)(2,1)S(1)} %copy-done.4), channel_id=1, source_target_pairs={{0,1},{1,0},{2,3},{3,2},{4,5},{5,4},{6,7},{7,6},{8,9},{9,8},{10,11... | collective-permute-start | bytes 1572872 | tf_op jit(solution)/shard_map/ppermute | solution.py:403
  94.7 30.5 %collective-permute-start.24 = (bf16[1024,256]{1,0:T(8,128)(2,1)S(1)}, bf16[1024,256]{1,0:T(8,128)(2,1)S(1)}, u32[]{:S(2)}, u32[]{:S(2)}) collective-permute-start(bf16[1024,256]{1,0:T(8,128)(2,1)S(1)} %collective-permute-done.10.refs_11_), channel_id=1, source_target_pairs={{0,1},{1,0},{2,3},{3,2},{4,5},{5,4},{6,7},{7,6},{8,9},{9,8},{10,11... | collective-permute-start | bytes 1572872 | tf_op jit(solution)/shard_map/ppermute | solution.py:403
  94.8 13.4 %collective-permute-start.18 = (bf16[64,1024]{1,0:T(8,128)(2,1)S(1)}, bf16[64,1024]{1,0:T(8,128)(2,1)S(1)}, u32[]{:S(2)}, u32[]{:S(2)}) collective-permute-start(bf16[64,1024]{1,0:T(8,128)(2,1)S(1)} %shard_map.85.refs_1_), channel_id=1, source_target_pairs={{8,0},{12,4},{16,8},{20,12},{24,16},{28,20},{0,24},{4,28},{9,1},{1... | collective-permute-start | bytes 393224 | tf_op jit(solution)/shard_map/ppermute | solution.py:412
  103.6 10.3 %collective-permute-start.19 = (bf16[64,1024]{1,0:T(8,128)(2,1)S(1)}, bf16[64,1024]{1,0:T(8,128)(2,1)S(1)}, u32[]{:S(2)}, u32[]{:S(2)}) collective-permute-start(bf16[64,1024]{1,0:T(8,128)(2,1)S(1)} %shard_map.85.refs_1_), channel_id=1, source_target_pairs={{24,0},{28,4},{0,8},{4,12},{8,16},{12,20},{16,24},{20,28},{25,1},{... | collective-permute-start | bytes 393224 | tf_op jit(solution)/shard_map/ppermute | solution.py:412
  103.6 10.3 %collective-permute-start.16 = (bf16[64,1024]{1,0:T(8,128)(2,1)S(1)}, bf16[64,1024]{1,0:T(8,128)(2,1)S(1)}, u32[]{:S(2)}, u32[]{:S(2)}) collective-permute-start(bf16[64,1024]{1,0:T(8,128)(2,1)S(1)} %shard_map.85.refs_1_), channel_id=1, source_target_pairs={{4,0},{8,4},{12,8},{16,12},{20,16},{24,20},{28,24},{0,28},{5,1},{9... | collective-permute-start | bytes 393224 | tf_op jit(solution)/shard_map/ppermute | solution.py:412
  108.2 11.1 %collective-permute-start.17 = (bf16[64,1024]{1,0:T(8,128)(2,1)S(1)}, bf16[64,1024]{1,0:T(8,128)(2,1)S(1)}, u32[]{:S(2)}, u32[]{:S(2)}) collective-permute-start(bf16[64,1024]{1,0:T(8,128)(2,1)S(1)} %shard_map.85.refs_1_), channel_id=1, source_target_pairs={{28,0},{0,4},{4,8},{8,12},{12,16},{16,20},{20,24},{24,28},{29,1},{... | collective-permute-start | bytes 393224 | tf_op jit(solution)/shard_map/ppermute | solution.py:412
  108.2 11.1 %collective-permute-start.20 = (bf16[64,1024]{1,0:T(8,128)(2,1)S(1)}, bf16[64,1024]{1,0:T(8,128)(2,1)S(1)}, u32[]{:S(2)}, u32[]{:S(2)}) collective-permute-start(bf16[64,1024]{1,0:T(8,128)(2,1)S(1)} %shard_map.85.refs_1_), channel_id=1, source_target_pairs={{16,0},{20,4},{24,8},{28,12},{0,16},{4,20},{8,24},{12,28},{17,1},{... | collective-permute-start | bytes 393224 | tf_op jit(solution)/shard_map/ppermute | solution.py:412
  113.9 8.1 %collective-permute-start.21 = (bf16[64,1024]{1,0:T(8,128)(2,1)S(1)}, bf16[64,1024]{1,0:T(8,128)(2,1)S(1)}, u32[]{:S(2)}, u32[]{:S(2)}) collective-permute-start(bf16[64,1024]{1,0:T(8,128)(2,1)S(1)} %collective-permute-done.18.refs_4_), channel_id=1, source_target_pairs={{4,0},{8,4},{12,8},{16,12},{20,16},{24,20},{28,24},{0,28},{5,1},{9... | collective-permute-start | bytes 393224 | tf_op jit(solution)/shard_map/ppermute | solution.py:412
  113.9 11.3 %collective-permute-start.22 = (bf16[64,1024]{1,0:T(8,128)(2,1)S(1)}, bf16[64,1024]{1,0:T(8,128)(2,1)S(1)}, u32[]{:S(2)}, u32[]{:S(2)}) collective-permute-start(bf16[64,1024]{1,0:T(8,128)(2,1)S(1)} %collective-permute-done.19.refs_5_), channel_id=1, source_target_pairs={{28,0},{0,4},{4,8},{8,12},{12,16},{16,20},{20,24},{24,28},{29,1},{... | collective-permute-start | bytes 393224 | tf_op jit(solution)/shard_map/ppermute | solution.py:412
  127.0 10.1 %collective-permute-start.25 = (bf16[2,64,1024]{2,1,0:T(8,128)(2,1)S(1)}, bf16[2,64,1024]{2,1,0:T(8,128)(2,1)S(1)}, u32[]{:S(2)}, u32[]{:S(2)}) collective-permute-start(bf16[2,64,1024]{2,1,0:T(8,128)(2,1)S(1)} %get-tuple-element.88), channel_id=1, source_target_pairs={{0,32},{32,64},{64,96},{96,0},{1,33},{33,65},{65,97},{97,1},{2,34}... | collective-permute-start | bytes 786440 | tf_op jit(solution)/shard_map/ppermute | solution.py:484
  127.1 16.5 %collective-permute-start.26 = (bf16[2,64,1024]{2,1,0:T(8,128)(2,1)S(1)}, bf16[2,64,1024]{2,1,0:T(8,128)(2,1)S(1)}, u32[]{:S(2)}, u32[]{:S(2)}) collective-permute-start(bf16[2,64,1024]{2,1,0:T(8,128)(2,1)S(1)} %get-tuple-element.89), channel_id=1, source_target_pairs={{0,64},{32,96},{64,0},{96,32},{1,65},{33,97},{65,1},{97,33},{2,66}... | collective-permute-start | bytes 786440 | tf_op jit(solution)/shard_map/ppermute | solution.py:484
  132.8 10.9 %collective-permute-start.27 = (bf16[2,64,1024]{2,1,0:T(8,128)(2,1)S(1)}, bf16[2,64,1024]{2,1,0:T(8,128)(2,1)S(1)}, u32[]{:S(2)}, u32[]{:S(2)}) collective-permute-start(bf16[2,64,1024]{2,1,0:T(8,128)(2,1)S(1)} %get-tuple-element.90), channel_id=1, source_target_pairs={{0,96},{32,0},{64,32},{96,64},{1,97},{33,1},{65,33},{97,65},{2,98}... | collective-permute-start | bytes 786440 | tf_op jit(solution)/shard_map/ppermute | solution.py:484
  143.8 3.9 %collective-permute-start.28 = (bf16[64,512]{1,0:T(8,128)(2,1)S(1)}, bf16[64,512]{1,0:T(8,128)(2,1)S(1)}, u32[]{:S(2)}, u32[]{:S(2)}) collective-permute-start(bf16[64,512]{1,0:T(8,128)(2,1)S(1)} %get-tuple-element.95), channel_id=1, source_target_pairs={{0,128},{2,130},{128,0},{130,2},{1,129},{3,131},{129,1},{131,3},{4... | collective-permute-start | bytes 196616 | tf_op jit(solution)/shard_map/ppermute | solution.py:493
  143.9 4.7 %collective-permute-start.29 = (bf16[64,512]{1,0:T(8,128)(2,1)S(1)}, bf16[64,512]{1,0:T(8,128)(2,1)S(1)}, u32[]{:S(2)}, u32[]{:S(2)}) collective-permute-start(bf16[64,512]{1,0:T(8,128)(2,1)S(1)} %get-tuple-element.97), channel_id=1, source_target_pairs={{0,2},{2,0},{128,130},{130,128},{1,3},{3,1},{129,131},{131,129},{4... | collective-permute-start | bytes 196616 | tf_op jit(solution)/shard_map/ppermute | solution.py:493
  144.0 5.4 %collective-permute-start.30 = (bf16[64,512]{1,0:T(8,128)(2,1)S(1)}, bf16[64,512]{1,0:T(8,128)(2,1)S(1)}, u32[]{:S(2)}, u32[]{:S(2)}) collective-permute-start(bf16[64,512]{1,0:T(8,128)(2,1)S(1)} %get-tuple-element.96), channel_id=1, source_target_pairs={{0,130},{2,128},{128,2},{130,0},{1,131},{3,129},{129,3},{131,1},{4... | collective-permute-start | bytes 196616 | tf_op jit(solution)/shard_map/ppermute | solution.py:493
  149.5 4.4 %collective-permute-start.31 = (bf16[2,64,256]{2,1,0:T(8,128)(2,1)S(1)}, bf16[2,64,256]{2,1,0:T(8,128)(2,1)S(1)}, u32[]{:S(2)}, u32[]{:S(2)}) collective-permute-start(bf16[2,64,256]{2,1,0:T(8,128)(2,1)S(1)} %pad_maximum_fusion.1), channel_id=1, source_target_pairs={{0,1},{1,0},{2,3},{3,2},{4,5},{5,4},{6,7},{7,6},{8,9},{9,8},{10,11... | collective-permute-start | bytes 196616 | tf_op jit(solution)/shard_map/ppermute | solution.py:403
